TPU v7x, 512 devices: a whole 4x4x16 slice. The times are simulated.
512 devices in a mesh: facet: 64 (over x_hi, z, core), col: 8 (over x_lo, y).
Axes of the slice: x: 4 (x_hi: 2, x_lo: 2; x = x_hi * 2 + x_lo), y: 4, z: 16, core: 2. Of those that a mesh axis runs over, the one named last changes fastest.
Arguments:
- facet_strips: bfloat16 [64, 2, 8192, 128], P('facet', None, 'col'), may hold values from -6 to 6
- facet_offsets: int32 [64, 2], P('facet'), may hold values from 0 to 65535
- column_offsets: int32 [8], P('col'), may hold values from 0 to 65535
- row_offsets: int32 [1], replicated, may hold values from 0 to 65535
- tile_lists: int32 [8, 64, 8], P('col', 'facet'), may hold values from 0 to 63
- tile_counts: int32 [8, 64], P('col', 'facet'), may hold values from 1 to 8, 256 in all within a row
- uv_index: int32 [8, 64, 8, 2, 1024], P('col', 'facet'), may hold values from 0 to 4095
Outputs:
- visibilities: float32 [8, 64, 8, 2, 1024], P('col', 'facet')
Inputs may be any that keep to these rules, and one draw needn't show every extreme that they name: `tile_counts`: each column has an owner whose count is exactly 8.
All inputs are finite; a program needn't handle non-finite values. No bound on the sum of `tile_counts` on one device may be relied on, other than what follows from the above.
Results may differ from a plain program's by a relative error of at most 0.0058.
Values may be sent and summed in bfloat16 or wider, within the bound.
A program may use at most 64 MiB of HBM per device.

v0:
```python
import math

import jax
import jax.numpy as jnp
from jax import lax
from jax.sharding import PartitionSpec as P

L = 8192
W = 128
S = 256
TILE = 32
NTOT = 65536
UV_STEPS = 4096


def copy_for_each(shard, axis):
    size = lax.axis_size(axis)
    return lax.all_to_all(
        jnp.broadcast_to(shard[None], (size, *shard.shape)), axis, 0, 0, tiled=True
    )


def over_copies(shard, axis):
    everything = copy_for_each(shard, axis)
    return jnp.sum(everything, axis=0)


def cut_along(shard, dim, size):
    shape = shard.shape
    parts = shard.reshape(*shape[:dim], size, shape[dim] // size, *shape[dim + 1 :])
    return jnp.moveaxis(parts, dim, 0)


def sent_and_summed(shard, axis, dim):
    parts = cut_along(shard, dim, lax.axis_size(axis))
    arrived = lax.all_to_all(parts, axis, split_axis=0, concat_axis=0, tiled=True)
    return arrived.sum(axis=0)


def in_order(parts, dim):
    parts = jnp.moveaxis(parts, 0, dim)
    shape = parts.shape
    return parts.reshape(*shape[:dim], shape[dim] * shape[dim + 1], *shape[dim + 2 :])


def gathered_copies(shard, axis, dim):
    parts = copy_for_each(shard, axis)
    return in_order(parts, dim)


def mod_product(first, second):
    high = first // 256
    low = first % 256
    return (high * (second * 256 % NTOT) + low * second) % NTOT


def phase_parts(row_start, row_count, row_step, col_start, col_count, col_step):
    left_side = ((row_start + row_step * jnp.arange(row_count, dtype=jnp.int32)) % NTOT)[:, None]
    right_side = ((col_start + col_step * jnp.arange(col_count, dtype=jnp.int32)) % NTOT)[None, :]
    index = mod_product(left_side, right_side)
    angle = index.astype(jnp.float32) * (2.0 * math.pi / NTOT)
    return (jnp.cos(angle), jnp.sin(angle))


def left_operator(row_start, col_start, count):
    cosine, sine = phase_parts(row_start, S, NTOT // L, col_start, count, 1)
    upper = jnp.concatenate([cosine, sine], axis=1)
    lower = jnp.concatenate([-sine, cosine], axis=1)
    return (jnp.concatenate([upper, lower], axis=0) * (1.0 / math.sqrt(L))).astype(jnp.bfloat16)


def right_operator(column_start, strip_start):
    cosine, sine = phase_parts(strip_start, W, 1, column_start, S, NTOT // S)
    table = jnp.stack([jnp.stack([cosine, -sine], axis=1), jnp.stack([sine, cosine], axis=1)])
    table = table * (1.0 / math.sqrt(W))
    return table.reshape(2, W, 2, S // TILE, TILE).astype(jnp.bfloat16)


def tile_terms(strip_rows, table):
    count = strip_rows.shape[0]
    shaped = strip_rows.reshape(count, 2, S // TILE, TILE, W)
    terms = jnp.einsum("rkapw,kwjbq->abrjpq", shaped, table, preferred_element_type=jnp.float32)
    return terms.reshape((S // TILE) ** 2, count, 2, TILE * TILE)


def visibilities_of(chosen, uv_slots):
    slots = chosen.shape[0]
    tiles = chosen.astype(jnp.float32).reshape(slots, 2, TILE, TILE)
    pixels = jnp.arange(TILE, dtype=jnp.int32)
    factor = 2.0 * math.pi / UV_STEPS
    u_angle = (uv_slots[:, 0, None, :] * pixels[None, :, None] % UV_STEPS).astype(
        jnp.float32
    ) * factor
    v_angle = (uv_slots[:, 1, None, :] * pixels[None, :, None] % UV_STEPS).astype(
        jnp.float32
    ) * factor
    u_cos, u_sin = (jnp.cos(u_angle), jnp.sin(u_angle))
    v_cos, v_sin = (jnp.cos(v_angle), jnp.sin(v_angle))
    high = lax.Precision.HIGHEST
    real_mid = jnp.einsum("cpq,cqk->cpk", tiles[:, 0], v_cos, precision=high) - jnp.einsum(
        "cpq,cqk->cpk", tiles[:, 1], v_sin, precision=high
    )
    imag_mid = jnp.einsum("cpq,cqk->cpk", tiles[:, 0], v_sin, precision=high) + jnp.einsum(
        "cpq,cqk->cpk", tiles[:, 1], v_cos, precision=high
    )
    real_vis = jnp.sum(u_cos * real_mid - u_sin * imag_mid, axis=1) / TILE
    imag_vis = jnp.sum(u_cos * imag_mid + u_sin * real_mid, axis=1) / TILE
    return jnp.stack([real_vis, imag_vis], axis=1)


def shards(
    facet_strips, facet_offsets, column_offsets, row_offsets, tile_lists, tile_counts, uv_index
):
    strip = facet_strips[0]
    strip_along = facet_offsets[0, 0]
    strip_across = facet_offsets[0, 1]
    row_total = row_offsets.shape[0]
    first_cell = lax.axis_index("col") * strip.shape[1]
    count = strip.shape[1]
    flat = strip.reshape(2 * count, strip.shape[2])
    parts = [
        jnp.dot(
            left_operator(row_offsets[0], strip_along + first_cell, count),
            flat,
            preferred_element_type=jnp.float32,
        )
    ]
    summed_rows = over_copies(jnp.stack(parts), "col")
    strip_rows = summed_rows.astype(jnp.bfloat16)
    table = right_operator(column_offsets[0], strip_across)
    terms = tile_terms(strip_rows, table) * (1.0 / math.sqrt(lax.axis_size("facet")))
    identity = tile_lists[0, 0]
    live = tile_counts[0, 0]
    slot_index = jnp.arange(identity.shape[0], dtype=jnp.int32)
    id_count = terms.shape[0] * row_total
    onehot = (
        (identity[:, None] == jnp.arange(id_count, dtype=jnp.int32)[None, :])
        & (slot_index[:, None] < live)
    ).astype(jnp.bfloat16)
    width = 2 * TILE * TILE
    owned = sent_and_summed(terms, "facet", 0).astype(jnp.bfloat16)
    piece = gathered_copies(owned, "facet", 0)
    count = piece.shape[0]
    flat = piece.reshape(count * row_total, width)
    chosen = jnp.dot(onehot, flat, preferred_element_type=jnp.float32)
    chosen = chosen.astype(jnp.bfloat16).reshape(identity.shape[0], 2, TILE * TILE)
    result = visibilities_of(chosen, uv_index[0, 0])
    return result[None, None]


def solution(mesh):
    in_specs = (
        P("facet", None, "col", None),
        P("facet", None),
        P("col"),
        P(),
        P("col", "facet", None),
        P("col", "facet"),
        P("col", "facet", None, None, None),
    )
    out_specs = P("col", "facet", None, None, None)
    return jax.shard_map(shards, mesh=mesh, in_specs=in_specs, out_specs=out_specs, check_vma=False)
```

profile of v0, /device:TPU:1, one launch (start us, length us, event | category | flops | bytes accessed | tf_op | source)
XLA Modules:
  0.0 155.9 jit_solution(3942736346510534915)
XLA Ops:
  0.0 0.0 copy-start
  0.0 1.3 fusion.76
  2.6 4.3 %fusion.19 = (f32[256,1024]{1,0:T(8,128)S(1)}, f32[256,1024]{1,0:T(8,128)S(1)}, f32[256,1024]{1,0:T(8,128)S(1)}) fusion(s32[1024]{0:T(1024)S(1)} %get-tuple-element.20, s32[256]{0:T(256)S(1)} %get-tuple-element.21, s32[1024]{0:T(1024)S(1)} %get-tuple-element.19, s32[256]{0:T(256)S(1)} %get-tuple-element.22), kind=kLoop, calls=%fused_computation.34 | loop fusion | flops 4456448 | bytes 3155968 | tf_op jit(solution)/shard_map/sin | solution.py:62
  6.9 0.0 copy-done
  6.9 0.7 fusion.2
  7.6 1.5 broadcast_in_dim.6
  9.1 6.0 %all-to-all-start = ((f32[8,1,512,128]{3,2,1,0:T(8,128)}), f32[8,1,512,128]{3,2,1,0:T(8,128)S(1)}, u32[]{:S(2)}, u32[]{:S(2)}) async-start(f32[8,1,512,128]{3,2,1,0:T(8,128)} %broadcast_in_dim.6), calls=%async_computation | async-start | bytes 4194304 | tf_op jit(solution)/shard_map/all_to_all | solution.py:18
  15.7 0.7 and_select_fusion.3
  16.4 0.6 fusion.41
  17.0 23.2 %all-to-all-done = f32[8,1,512,128]{3,2,1,0:T(8,128)S(1)} async-done(((f32[8,1,512,128]{3,2,1,0:T(8,128)}), f32[8,1,512,128]{3,2,1,0:T(8,128)S(1)}, u32[]{:S(2)}, u32[]{:S(2)}) %all-to-all-start) | async-done | bytes 2097184 | tf_op jit(solution)/shard_map/all_to_all | solution.py:18
  40.1 0.1 reduce_sum.36
  40.2 1.8 %fusion.1 = f32[8,8,1,2,32,32]{4,5,0,1,3,2:T(8,128)} fusion(bf16[2,8,32,128,1,1]{3,2,1,0,5,4:T(8,128)(2,1)S(1)} %bitcast.67, f32[1,128,1,8,32]{1,4,0,3,2:T(8,128)S(1)} %get-tuple-element.14, f32[1,128,1,8,32]{1,4,0,3,2:T(8,128)S(1)} %get-tuple-element.13, f32[1,128,1,8,32]{1,4,0,3,2:T(8,128)S(1)} %get-tuple-element.12), kind=kOutput, calls=%fused_computation.4 | convolution fusion | flops 67895296 | bytes 1048576 | tf_op jit(solution)/shard_map/rkapw,kwjbq->abrjpq/dot_general | solution.py:82
  42.0 1.9 %copy.33 = f32[8,8,1,2,32,32]{5,4,3,1,0,2:T(8,128)S(1)} copy(f32[8,8,1,2,32,32]{4,5,0,1,3,2:T(8,128)} %fusion.1) | data formatting | bytes 1048576 | tf_op jit(solution)/shard_map/mul | solution.py:131
  44.0 0.0 copy-start.1
  44.0 1.1 reshape.510
  45.1 0.0 copy-start.2
  45.1 52.6 %all_to_all.15 = f32[64,1,1,2,1024]{4,3,2,1,0:T(2,128)S(1)} all-to-all(f32[64,1,1,2,1024]{4,3,2,1,0:T(2,128)S(1)} %reshape.510), channel_id=1, replica_groups=mesh['facet'=64,'col'=8] {'facet'}, dimensions={0} | all-to-all | bytes 1048576 | tf_op jit(solution)/shard_map/all_to_all | solution.py:36
  97.8 0.2 reduce_sum.37
  98.0 0.8 broadcast_in_dim.7
  98.8 5.9 %all-to-all-start.2 = ((bf16[64,1,1,2,1024]{4,3,2,1,0:T(2,128)(2,1)}), bf16[64,1,1,2,1024]{4,3,2,1,0:T(2,128)(2,1)S(1)}, u32[]{:S(2)}, u32[]{:S(2)}) async-start(bf16[64,1,1,2,1024]{4,3,2,1,0:T(2,128)(2,1)} %broadcast_in_dim.7), calls=%async_computation.2 | async-start | bytes 524288 | tf_op jit(solution)/shard_map/all_to_all | solution.py:18
  105.3 0.0 copy-done.1
  105.3 0.1 fusion.75
  105.4 23.0 %all-to-all-done.2 = bf16[64,1,1,2,1024]{4,3,2,1,0:T(2,128)(2,1)S(1)} async-done(((bf16[64,1,1,2,1024]{4,3,2,1,0:T(2,128)(2,1)}), bf16[64,1,1,2,1024]{4,3,2,1,0:T(2,128)(2,1)S(1)}, u32[]{:S(2)}, u32[]{:S(2)}) %all-to-all-start.2) | async-done | bytes 262176 | tf_op jit(solution)/shard_map/all_to_all | solution.py:18
  128.4 0.1 copy.39
  128.5 0.0 copy-done.2
  128.5 0.2 convolution_convert_fusion
  128.7 0.2 reshape.506
  128.9 5.6 %fusion.25 = f32[8,32,1024]{2,1,0:T(8,128)S(1)} fusion(s32[8,1024]{1,0:T(8,128)S(1)} %get-tuple-element.17, bf16[8,2,32,32]{3,2,1,0:T(8,128)(2,1)S(1)} %reshape.506), kind=kOutput, calls=%fused_computation.40 | convolution fusion | flops 104333312 | bytes 1146880 | tf_op jit(solution)/shard_map/cpq,cqk->cpk/dot_general | solution.py:100
  134.5 5.6 %fusion.27 = f32[8,32,1024]{2,1,0:T(8,128)S(1)} fusion(s32[8,1024]{1,0:T(8,128)S(1)} %get-tuple-element.17, bf16[8,2,32,32]{3,2,1,0:T(8,128)(2,1)S(1)} %reshape.506), kind=kOutput, calls=%fused_computation.41 | convolution fusion | flops 104333312 | bytes 1146880 | tf_op jit(solution)/shard_map/cpq,cqk->cpk/dot_general | solution.py:103
  140.1 5.7 %convolution_subtract_fusion = f32[8,32,1024]{2,1,0:T(8,128)S(1)} fusion(f32[8,32,1024]{2,1,0:T(8,128)S(1)} %fusion.25, s32[8,1024]{1,0:T(8,128)S(1)} %get-tuple-element.17, bf16[8,2,32,32]{3,2,1,0:T(8,128)(2,1)S(1)} %reshape.506), kind=kOutput, calls=%fused_computation.16 | convolution fusion | flops 104595456 | bytes 2195456 | tf_op jit(solution)/shard_map/cpq,cqk->cpk/dot_general | solution.py:100
  145.8 9.3 %subtract_reduce_fusion = (f32[8,1024]{1,0:T(8,128)S(1)}, f32[8,1024]{1,0:T(8,128)S(1)}) fusion(f32[8,32,1024]{2,1,0:T(8,128)S(1)} %convolution_subtract_fusion, s32[8,1024]{1,0:T(8,128)S(1)} %get-tuple-element.18, f32[8,32,1024]{2,1,0:T(8,128)S(1)} %fusion.27, s32[8,1024]{1,0:T(8,128)S(1)} %get-tuple-element.17, bf16[8,2,32,32]{3,2,1,0:T(8,128)(2,1)S(1)} %reshape.506), kind=kOutput, calls=%fused_computation.27 | convolution fusion | flops 110346240 | bytes 2293760 | tf_op jit(solution)/shard_map/cpq,cqk->cpk/dot_general | solution.py:103
  155.2 0.7 maximum_bitcast_fusion
  (9 shorter events, 0.2 us)
Async XLA Ops:
  0.0 6.9 %copy-start = (bf16[1,2,1024,128]{3,2,1,0:T(8,128)(2,1)S(1)}, bf16[1,2,1024,128]{3,2,1,0:T(8,128)(2,1)}, u32[]{:S(2)}) copy-start(bf16[1,2,1024,128]{3,2,1,0:T(8,128)(2,1)} %param.7) | copy-start | bytes 1572868
  9.1 31.1 %all-to-all-start = ((f32[8,1,512,128]{3,2,1,0:T(8,128)}), f32[8,1,512,128]{3,2,1,0:T(8,128)S(1)}, u32[]{:S(2)}, u32[]{:S(2)}) async-start(f32[8,1,512,128]{3,2,1,0:T(8,128)} %broadcast_in_dim.6), calls=%async_computation | async-start | bytes 4194304 | tf_op jit(solution)/shard_map/all_to_all | solution.py:18
  44.0 61.4 %copy-start.1 = (s32[1,1,8,2,1024]{4,3,2,1,0:T(2,128)S(1)}, s32[1,1,8,2,1024]{4,3,2,1,0:T(2,128)}, u32[]{:S(2)}) copy-start(s32[1,1,8,2,1024]{4,3,2,1,0:T(2,128)} %param.13) | copy-start | bytes 196612
  45.1 83.4 %copy-start.2 = (s32[1,1,8]{2,1,0:T(1,128)S(1)}, s32[1,1,8]{2,1,0:T(1,128)}, u32[]{:S(2)}) copy-start(s32[1,1,8]{2,1,0:T(1,128)} %param.11) | copy-start | bytes 100
  98.8 29.6 %all-to-all-start.2 = ((bf16[64,1,1,2,1024]{4,3,2,1,0:T(2,128)(2,1)}), bf16[64,1,1,2,1024]{4,3,2,1,0:T(2,128)(2,1)S(1)}, u32[]{:S(2)}, u32[]{:S(2)}) async-start(bf16[64,1,1,2,1024]{4,3,2,1,0:T(2,128)(2,1)} %broadcast_in_dim.7), calls=%async_computation.2 | async-start | bytes 524288 | tf_op jit(solution)/shard_map/all_to_all | solution.py:18
where the time goes:
time: 156 us
  blocking collectives  52.6 us (34%)
  waiting for transfers between devices  46.1 us (30%)
  matrix products  29 us (19%)
  starting transfers between devices  11.8 us (8%)
  local copies, waits for them, and re-layouts  7.04 us (5%)
  other arithmetic  6.64 us (4%)
  between operations  2.71 us (2%)
    all_to_all x1, blocking collectives, sent_and_summed(): lax.all_to_all(parts, axis, split_axis=0, concat_axis=0, tiled=True)  52.6 us
    all_to_all x2, waiting for transfers between devices, copy_for_each(): lax.all_to_all(jnp.broadcast_to(shard[None], (size, *shard.shape)), axis,...  46.1 us
    all_to_all x2, starting transfers between devices, copy_for_each(): lax.all_to_all(jnp.broadcast_to(shard[None], (size, *shard.shape)), axis,...  11.8 us
    dot_general x1, matrix products, visibilities_of(): jnp.einsum('cpq,cqk->cpk', tiles[:, 1], v_cos, precision=high)  9.35 us
    dot_general x1, matrix products, visibilities_of(): jnp.einsum('cpq,cqk->cpk', tiles[:, 1], v_sin, precision=high)  5.65 us
    dot_general x1, matrix products, visibilities_of(): jnp.einsum('cpq,cqk->cpk', tiles[:, 0], v_sin, precision=high)  5.63 us
    dot_general x1, matrix products, visibilities_of(): jnp.einsum('cpq,cqk->cpk', tiles[:, 0], v_cos, precision=high)  5.61 us
    sin x1, other arithmetic, phase_parts(): return (jnp.cos(angle), jnp.sin(angle))  4.27 us
  transfers between devices with their start and end apart: 2, of which 2 were waited for; matrix products, arithmetic and copies ran while one was open for 1% of the time, Pallas kernels for 0%

commit v1 on v0

v1 whole, which is shorter than its diff:
```python
import math

import jax
import jax.numpy as jnp
from jax import lax
from jax.experimental import pallas as pl
from jax.experimental.pallas import tpu as pltpu
from jax.sharding import PartitionSpec as P

L = 8192
W = 128
S = 256
TILE = 32
NTOT = 65536
UV_STEPS = 4096
VIS = 1024
CAP = 8
FACETS = 64
LEN = 1024
MESH = pl.DeviceIdType.MESH
F32 = jnp.float32
BF16 = jnp.bfloat16
I32 = jnp.int32


def unit(index):
    index = index & (NTOT - 1)
    index = jnp.where(index >= NTOT // 2, index - NTOT, index)
    angle = index.astype(F32) * (2.0 * math.pi / NTOT)
    return jnp.cos(angle), jnp.sin(angle)


def cmul(a, b):
    return a[0] * b[0] - a[1] * b[1], a[0] * b[1] + a[1] * b[0]


def iota(shape, dim):
    return lax.broadcasted_iota(I32, shape, dim)


def facet_of(x_hi, z, core):
    return (x_hi * 16 + z) * 2 + core


def group_facet(g, zg):
    return facet_of(g // 4, 2 * zg + g % 2, (g // 2) % 2)


def kernel(
    strip_ref,
    offsets_ref,
    column_ref,
    row_ref,
    lists_ref,
    counts_ref,
    uv_ref,
    out_ref,
    strip_v,
    uv_v,
    left_v,
    send1,
    recv1,
    block2,
    recv2,
    table_v,
    send3,
    recv3,
    recv4,
    small_v,
    recv_s,
    pick_v,
    send5,
    recv5,
    pow_v,
    u_v,
    v_v,
    load_sem,
    s_s,
    r_s,
    s_1,
    r_1,
    s_2,
    r_2,
    s_3,
    r_3,
    s_4,
    r_4,
    s_5,
    r_5,
):
    facet = lax.axis_index("facet")
    col = lax.axis_index("col")
    x_hi = facet // 32
    z = (facet // 2) % 16
    core = facet % 2
    zg = z // 2
    zp = z % 2
    q_me = x_hi * 2 + core
    g_me = q_me * 2 + zp
    place = 8 * zp + zg

    loads = [
        pltpu.make_async_copy(strip_ref.at[0, 0], strip_v.at[:, pl.ds(0, W)], load_sem.at[0]),
        pltpu.make_async_copy(strip_ref.at[0, 1], strip_v.at[:, pl.ds(W, W)], load_sem.at[1]),
        pltpu.make_async_copy(uv_ref.at[0, 0], uv_v, load_sem.at[2]),
    ]
    for load in loads:
        load.start()

    barrier = pltpu.get_barrier_semaphore()

    def greet(f, c):
        pl.semaphore_signal(barrier, inc=1, device_id=(f, c), device_id_type=MESH)

    @pl.loop(1, 8)
    def _(i):
        greet(facet, (col + i) % 8)

    @pl.loop(1, 8)
    def _(i):
        greet(group_facet((g_me + i) % 8, zg), col)

    @pl.loop(1, 16)
    def _(i):
        @pl.when((z + i) % 16 != 2 * zg + (1 - zp))
        def _():
            greet(facet_of(x_hi, (z + i) % 16, core), col)

    @pl.when(col != g_me)
    def _():
        @pl.loop(0, 8)
        def _(g):
            greet(group_facet(g, zg), g_me)

    row0 = row_ref[0]
    cells = offsets_ref[0, 0] + col * LEN + iota((8, LEN), 1)
    base = unit((row0 + 8 * iota((8, LEN), 0)) * cells)
    scale = 1.0 / math.sqrt(L)
    step = unit(64 * cells)

    def left_body(t, value):
        nxt = cmul(value, step)
        at = pl.ds(pl.multiple_of(16 * t, 16), 16)
        left_v[at, :] = jnp.concatenate([value[0], nxt[0]], axis=0).astype(BF16)
        at = pl.ds(pl.multiple_of(S + 16 * t, 16), 16)
        left_v[at, :] = jnp.concatenate([value[1], nxt[1]], axis=0).astype(BF16)
        return cmul(nxt, step)

    lax.fori_loop(0, 16, left_body, (base[0] * scale, base[1] * scale))

    loads[0].wait()
    loads[1].wait()
    both = jnp.dot(left_v[...], strip_v[...], preferred_element_type=F32)
    real = both[:S, :W] + both[S:, W:]
    imag = both[:S, W:] - both[S:, :W]
    send1[...] = jnp.concatenate([real, imag], axis=1).astype(BF16).reshape(8, 32, 2 * W)

    pl.semaphore_wait(barrier, 35)

    def copy1(c):
        return pltpu.make_async_remote_copy(
            src_ref=send1.at[c], dst_ref=recv1.at[col], send_sem=s_1.at[c], recv_sem=r_1.at[col],
            device_id=(facet, c), device_id_type=MESH,
        )

    def from1(c):
        return pltpu.make_async_remote_copy(
            src_ref=send1.at[c], dst_ref=recv1.at[c], send_sem=s_1.at[c], recv_sem=r_1.at[c],
            device_id=(facet, c), device_id_type=MESH,
        )

    @pl.loop(1, 8)
    def _(i):
        copy1((col + i) % 8).start()

    recv1[pl.ds(col, 1)] = send1[pl.ds(col, 1)]

    lanes = iota((8, W), 0)
    ids = jnp.full((8, W), -1, I32)
    for j in range(CAP):
        ids = jnp.where((lanes == j) & (j < counts_ref[0, 0]), lists_ref[0, 0, j], ids)
    small_v[0:8, :] = ids
    small_v[8:16, :] = jnp.full((8, W), offsets_ref[0, 1], I32)
    recv_s[pl.ds(g_me, 1)] = small_v[...][None]

    def copy_s(g, dst):
        return pltpu.make_async_remote_copy(
            src_ref=small_v, dst_ref=recv_s.at[dst], send_sem=s_s.at[g], recv_sem=r_s.at[dst],
            device_id=(group_facet(g, zg), col), device_id_type=MESH,
        )

    @pl.loop(1, 8)
    def _(i):
        copy_s((g_me + i) % 8, g_me).start()

    lane = iota((8, 2 * S), 1)
    sample = column_ref[0] + 256 * (32 * (lane // 64) + lane % 32)
    quarter = (NTOT // 4) * ((lane // 32) % 2)
    base_r = unit(iota((8, 2 * S), 0) * sample + quarter)
    step_r = unit(8 * sample)

    def right_body(t, value):
        nxt = cmul(value, step_r)
        re = jnp.concatenate([value[0], nxt[0]], axis=0)
        im = jnp.concatenate([value[1], nxt[1]], axis=0)
        top = pl.ds(pl.multiple_of(16 * t, 16), 16)
        low = pl.ds(pl.multiple_of(W + 16 * t, 16), 16)
        table_v[top, 0 : 2 * S] = re.astype(BF16)
        table_v[low, 0 : 2 * S] = im.astype(BF16)
        table_v[top, 2 * S :] = (-im).astype(BF16)
        table_v[low, 2 * S :] = re.astype(BF16)
        return cmul(nxt, step_r)

    lax.fori_loop(0, 8, right_body, base_r)

    @pl.loop(1, 8)
    def _(i):
        from1((col + i) % 8).wait_recv()

    total = recv1[0].astype(F32)
    for c in range(1, 8):
        total = total + recv1[c].astype(F32)
    block2[...] = total.astype(BF16)

    def copy2(c):
        return pltpu.make_async_remote_copy(
            src_ref=block2, dst_ref=recv2.at[g_me], send_sem=s_2.at[c], recv_sem=r_2.at[g_me],
            device_id=(group_facet(col, zg), c), device_id_type=MESH,
        )

    def from2(g):
        return pltpu.make_async_remote_copy(
            src_ref=block2, dst_ref=recv2.at[g], send_sem=s_2.at[g], recv_sem=r_2.at[g],
            device_id=(group_facet(g, zg), g_me), device_id_type=MESH,
        )

    @pl.when(col == g_me)
    def _():
        recv2[pl.ds(g_me, 1)] = block2[...][None]

    @pl.when(col != g_me)
    def _():
        copy2(col).start()

    @pl.loop(1, 8)
    def _(i):
        copy2((col + i) % 8).start()

    loads[2].wait()
    for part in range(2):
        index = jnp.concatenate([uv_v[j, part : part + 1, :] for j in range(CAP)], axis=0)
        value = unit(index * (NTOT // UV_STEPS))
        for k in range(5):
            pow_v[part, k, 0] = value[0]
            pow_v[part, k, 1] = value[1]
            value = cmul(value, value)

    sub = iota((8, VIS), 0)

    def powers(part, j):
        def power(k):
            return tuple(
                jnp.broadcast_to(pow_v[part, k, h, pl.ds(j, 1), :], (8, VIS)) for h in range(2)
            )

        def chosen_power(k):
            re, im = power(k)
            on = (sub & (1 << k)) != 0
            return jnp.where(on, re, 1.0), jnp.where(on, im, 0.0)

        low = cmul(cmul(chosen_power(0), chosen_power(1)), chosen_power(2))
        sixteen = power(4)
        second = cmul(low, power(3))
        third = cmul(low, sixteen)
        fourth = cmul(second, sixteen)
        parts = (low, second, third, fourth)
        return tuple(jnp.concatenate([p[h] for p in parts], axis=0) for h in range(2))

    @pl.loop(0, CAP)
    def _(j):
        re, im = powers(0, j)
        u_v[0, j] = re * (1.0 / TILE)
        u_v[1, j] = im * (1.0 / TILE)
        re, im = powers(1, j)
        top = pl.ds(pl.multiple_of(64 * j, 32), 32)
        low = pl.ds(pl.multiple_of(64 * j + 32, 32), 32)
        v_v[top, 0:VIS] = re.astype(BF16)
        v_v[top, VIS:] = im.astype(BF16)
        v_v[low, 0:VIS] = (-im).astype(BF16)
        v_v[low, VIS:] = re.astype(BF16)

    @pl.loop(1, 8)
    def _(i):
        copy_s((g_me + i) % 8, (g_me + i) % 8).wait_recv()

    across = jnp.zeros((8, W), I32)
    for g in range(8):
        across = jnp.where(lanes == g, recv_s[g, 8:16, :], across)
    across = jnp.concatenate([across] * 4, axis=1)
    turn = unit(across * sample)
    norm = 1.0 / math.sqrt(W * FACETS)
    turn = (turn[0] * norm, turn[1] * norm)

    entry = iota((16, 2 * W), 1)
    diagonal = iota((16, 2 * W), 0) == entry % 16
    entry = 16 * q_me + entry // 16

    @pl.loop(0, 4)
    def _(q):
        for j in range(CAP):
            wanted = recv_s[2 * q + zp, j : j + 1, :]
            wanted = jnp.broadcast_to(jnp.concatenate([wanted, wanted], axis=1), (16, 2 * W))
            pick = jnp.where((wanted == entry) & diagonal, 1.0, 0.0)
            pick_v[q, 16 * j : 16 * j + 16, :] = pick.astype(BF16)

    @pl.when(col == g_me)
    def _():
        @pl.loop(1, 8)
        def _(i):
            from2((g_me + i) % 8).wait_recv()

    @pl.when(col != g_me)
    def _():
        @pl.loop(0, 8)
        def _(g):
            from2(g).wait_recv()

    grid = jnp.dot(
        recv2[...].reshape(8 * 32, 2 * W), table_v[...], preferred_element_type=F32
    )
    terms = None
    for g in range(8):
        rows = grid[32 * g : 32 * g + 32]
        term = rows[:, : 2 * S] * turn[0][g : g + 1] + rows[:, 2 * S :] * turn[1][g : g + 1]
        terms = term if terms is None else terms + term

    low_half = iota((16, W), 1) < 64
    for v in range(4):
        top = terms[0:16, W * v : W * v + W]
        low = terms[16:32, W * v : W * v + W]
        send3[2 * v] = jnp.where(low_half, top, pltpu.roll(low, 64, 1)).astype(BF16)
        send3[2 * v + 1] = jnp.where(low_half, pltpu.roll(top, 64, 1), low).astype(BF16)

    def copy3(b, dst):
        return pltpu.make_async_remote_copy(
            src_ref=send3.at[b], dst_ref=recv3.at[dst], send_sem=s_3.at[b], recv_sem=r_3.at[dst],
            device_id=(facet_of(x_hi, 2 * b + zp, core), col), device_id_type=MESH,
        )

    @pl.loop(1, 8)
    def _(i):
        copy3((zg + i) % 8, zg).start()

    recv3[pl.ds(zg, 1)] = send3[pl.ds(zg, 1)]

    @pl.loop(1, 8)
    def _(i):
        copy3((zg + i) % 8, (zg + i) % 8).wait_recv()

    total = recv3[0].astype(F32)
    for b in range(1, 8):
        total = total + recv3[b].astype(F32)
    recv4[pl.ds(place, 1)] = total.astype(BF16)[None]

    def copy4(n, dst):
        return pltpu.make_async_remote_copy(
            src_ref=recv4.at[place], dst_ref=recv4.at[dst], send_sem=s_4.at[n], recv_sem=r_4.at[dst],
            device_id=(facet_of(x_hi, 2 * (n % 8) + n // 8, core), col), device_id_type=MESH,
        )

    @pl.loop(1, 16)
    def _(i):
        copy4((place + i) % 16, place).start()

    @pl.loop(1, 16)
    def _(i):
        copy4((place + i) % 16, (place + i) % 16).wait_recv()

    picks = jnp.dot(
        pick_v[...].reshape(4 * W, 2 * W), recv4[...].reshape(2 * W, W), preferred_element_type=F32
    )
    send5[...] = picks.astype(BF16).reshape(4, W, W)

    def copy5(q, dst):
        return pltpu.make_async_remote_copy(
            src_ref=send5.at[q], dst_ref=recv5.at[dst], send_sem=s_5.at[q], recv_sem=r_5.at[dst],
            device_id=(facet_of(q // 2, z, q % 2), col), device_id_type=MESH,
        )

    @pl.loop(1, 4)
    def _(i):
        copy5((q_me + i) % 4, q_me).start()

    recv5[pl.ds(q_me, 1)] = send5[pl.ds(q_me, 1)]

    @pl.loop(1, 4)
    def _(i):
        copy5((q_me + i) % 4, (q_me + i) % 4).wait_recv()

    chosen = recv5[0].astype(F32)
    for q in range(1, 4):
        chosen = chosen + recv5[q].astype(F32)

    for h in range(2):
        rows = []
        for i in range(4):
            tile = chosen[64 * h + 16 * i : 64 * h + 16 * i + 16]
            other = pltpu.roll(tile, 64, 1)
            if i % 2 == 0:
                top, low = jnp.where(low_half, tile, 0.0), jnp.where(low_half, other, 0.0)
            else:
                top, low = jnp.where(low_half, 0.0, other), jnp.where(low_half, 0.0, tile)
            here = jnp.concatenate([top, low], axis=0)
            none = jnp.zeros_like(here)
            rows.append(jnp.concatenate([here, none] if i < 2 else [none, here], axis=1))
        lhs = jnp.concatenate(rows, axis=0).astype(BF16)
        deep = slice(256 * h, 256 * h + 256)
        for k in range(0, VIS, 256):
            re = jnp.dot(lhs, v_v[deep, k : k + 256], preferred_element_type=F32)
            im = jnp.dot(lhs, v_v[deep, VIS + k : VIS + k + 256], preferred_element_type=F32)
            for i in range(4):
                j = 4 * h + i
                a = (re[32 * i : 32 * i + 32], im[32 * i : 32 * i + 32])
                b = (u_v[0, j, :, k : k + 256], u_v[1, j, :, k : k + 256])
                vis = cmul(a, b)
                for part in range(2):
                    out_ref[0, 0, j, part : part + 1, k : k + 256] = jnp.sum(
                        vis[part], axis=0, keepdims=True
                    )

    @pl.loop(1, 8)
    def _(i):
        copy1((col + i) % 8).wait_send()
        copy_s((g_me + i) % 8, g_me).wait_send()
        copy2((col + i) % 8).wait_send()
        copy3((zg + i) % 8, zg).wait_send()

    @pl.when(col != g_me)
    def _():
        copy2(col).wait_send()

    @pl.loop(1, 16)
    def _(i):
        copy4((place + i) % 16, place).wait_send()

    @pl.loop(1, 4)
    def _(i):
        copy5((q_me + i) % 4, q_me).wait_send()


def shards(
    facet_strips, facet_offsets, column_offsets, row_offsets, tile_lists, tile_counts, uv_index
):
    smem = pl.BlockSpec(memory_space=pltpu.SMEM)
    anywhere = pl.BlockSpec(memory_space=pl.ANY)
    dma = pltpu.SemaphoreType.DMA
    return pl.pallas_call(
        kernel,
        out_shape=jax.ShapeDtypeStruct((1, 1, CAP, 2, VIS), F32),
        in_specs=[anywhere, smem, smem, smem, smem, smem, anywhere],
        out_specs=pl.BlockSpec(memory_space=pltpu.VMEM),
        scratch_shapes=[
            pltpu.VMEM((LEN, 2 * W), BF16),
            pltpu.VMEM((CAP, 2, VIS), I32),
            pltpu.VMEM((2 * S, LEN), BF16),
            pltpu.VMEM((8, 32, 2 * W), BF16),
            pltpu.VMEM((8, 32, 2 * W), BF16),
            pltpu.VMEM((32, 2 * W), BF16),
            pltpu.VMEM((8, 32, 2 * W), BF16),
            pltpu.VMEM((2 * W, 4 * S), BF16),
            pltpu.VMEM((8, 16, W), BF16),
            pltpu.VMEM((8, 16, W), BF16),
            pltpu.VMEM((16, 16, W), BF16),
            pltpu.VMEM((16, W), I32),
            pltpu.VMEM((8, 16, W), I32),
            pltpu.VMEM((4, W, 2 * W), BF16),
            pltpu.VMEM((4, W, W), BF16),
            pltpu.VMEM((4, W, W), BF16),
            pltpu.VMEM((2, 5, 2, CAP, VIS), F32),
            pltpu.VMEM((2, CAP, TILE, VIS), F32),
            pltpu.VMEM((CAP * 64, 2 * VIS), BF16),
            dma((3,)),
            dma((8,)),
            dma((8,)),
            dma((8,)),
            dma((8,)),
            dma((8,)),
            dma((8,)),
            dma((8,)),
            dma((8,)),
            dma((16,)),
            dma((16,)),
            dma((4,)),
            dma((4,)),
        ],
        compiler_params=pltpu.CompilerParams(
            collective_id=0, has_side_effects=True, vmem_limit_bytes=48 * 1024 * 1024
        ),
    )(facet_strips, facet_offsets, column_offsets, row_offsets, tile_lists, tile_counts, uv_index)


def solution(mesh):
    in_specs = (
        P("facet", None, "col", None),
        P("facet", None),
        P("col"),
        P(),
        P("col", "facet", None),
        P("col", "facet"),
        P("col", "facet", None, None, None),
    )
    out_specs = P("col", "facet", None, None, None)
    return jax.shard_map(shards, mesh=mesh, in_specs=in_specs, out_specs=out_specs, check_vma=False)
```

time: 156 us -> 55 us (0.35)
  blocking collectives: 52.6 us -> 0 us
  Pallas kernels: 0 us -> 50.3 us
  waiting for transfers between devices: 46.1 us -> 0 us
  matrix products: 29 us -> 0 us
  starting transfers between devices: 11.8 us -> 0 us
  other arithmetic: 6.64 us -> 0 us
  local copies, waits for them, and re-layouts: 7.04 us -> 2.51 us
    all_to_all x1 -> x0, blocking collectives: 52.6 us -> none  [sent_and_summed(): lax.all_to_all(parts, axis, split_axis=0, concat_axis=0, tiled=True)]
    pallas_call x0 -> x1, Pallas kernels: none -> 50.3 us  [shards(): pl.pallas_call(kernel, out_shape=jax.ShapeDtypeStruct((1, 1, CAP, 2, VIS)...]
    all_to_all x2 -> x0, waiting for transfers between devices: 46.1 us -> none  [copy_for_each(): lax.all_to_all(jnp.broadcast_to(shard[None], (size, *shard.shape)), axis,...]
    dot_general x7 -> x0, matrix products: 29 us -> none  [the longest x1 9.35 us: visibilities_of(): jnp.einsum('cpq,cqk->cpk', tiles[:, 1], v_cos, precision=high)]
    all_to_all x2 -> x0, starting transfers between devices: 11.8 us -> none  [copy_for_each(): lax.all_to_all(jnp.broadcast_to(shard[None], (size, *shard.shape)), axis,...]
    sin x1 -> x0, other arithmetic: 4.27 us -> none  [phase_parts(): return (jnp.cos(angle), jnp.sin(angle))]
    mul x2 -> x0, local copies, waits for them, and re-layouts: 3.06 us -> none  [shards(): tile_terms(strip_rows, table) * (1.0 / math.sqrt(lax.axis_size('facet')))]
    unnamed x8 -> x9, local copies, waits for them, and re-layouts: 0.08 us -> 2.51 us
  transfers between devices with their start and end apart: 2 -> 0, of which waited for: 2 -> 0; matrix products, arithmetic and copies ran while one was open for 1% -> 0% of each run, Pallas kernels for 0% -> 0%
where the time goes in v1:
time: 55 us; the launch traced here: 54.8 us
  Pallas kernels  50.3 us (91%)
  local copies, waits for them, and re-layouts  2.51 us (5%)
  between operations  2.01 us (4%)
    pallas_call x1, Pallas kernels, shards(): pl.pallas_call(kernel, out_shape=jax.ShapeDtypeStruct((1, 1, CAP, 2, VIS)...  50.3 us
    unnamed x9, local copies, waits for them, and re-layouts  2.51 us

profile of v1, /device:TPU:1, one launch (start us, length us, event | category | flops | bytes accessed | tf_op | source)
XLA Modules:
  0.0 54.8 jit_solution(8861997817691066527)
XLA Ops:
  1.3 0.0 copy-start.2
  1.3 0.0 copy-start.3
  2.0 0.0 copy-done.2
  2.0 0.0 copy-done.3
  2.0 0.0 copy-start
  2.0 1.0 %copy-done = bf16[1,2,1024,128]{3,2,1,0:T(8,128)(2,1)S(1)} copy-done((bf16[1,2,1024,128]{3,2,1,0:T(8,128)(2,1)S(1)}, bf16[1,2,1024,128]{3,2,1,0:T(8,128)(2,1)}, u32[]{:S(2)}) %copy-start) | copy-done | bytes 524312
  3.0 0.0 copy-start.1
  3.0 0.8 %copy-done.1 = s32[1,1,8,2,1024]{4,3,2,1,0:T(2,128)S(1)} copy-done((s32[1,1,8,2,1024]{4,3,2,1,0:T(2,128)S(1)}, s32[1,1,8,2,1024]{4,3,2,1,0:T(2,128)}, u32[]{:S(2)}) %copy-start.1) | copy-done | bytes 65560
  3.9 50.3 %shard_map.73 = f32[1,1,8,2,1024]{4,3,2,1,0:T(2,128)S(1)} custom-call(bf16[1,2,1024,128]{3,2,1,0:T(8,128)(2,1)S(1)} %copy-done, s32[1,2]{1,0:T(1,128)S(1)} %copy-done.2, s32[1]{0:T(128)S(6)} %copy.9.column_ref, s32[1]{0:T(128)S(6)} %copy.10.row_ref, s32[1,1,8]{2,1,0:T(1,128)S(1)} %copy-done.3, s32[1,1]{1,0:T(1,128)S(6)} %copy.11.counts_ref, ...), custom_call_target="tpu_custom_call" | custom-call | tf_op jit(solution)/shard_map/pallas_call | solution.py:457
  54.1 0.6 %copy.12 = f32[1,1,8,2,1024]{4,3,2,1,0:T(2,128)} copy(f32[1,1,8,2,1024]{4,3,2,1,0:T(2,128)S(1)} %shard_map.73) | data formatting | bytes 131072
Async XLA Ops:
  1.3 0.7 %copy-start.2 = (s32[1,2]{1,0:T(1,128)S(1)}, s32[1,2]{1,0:T(1,128)}, u32[]{:S(2)}) copy-start(s32[1,2]{1,0:T(1,128)} %offsets_ref.1) | copy-start | bytes 28
  1.3 0.7 %copy-start.3 = (s32[1,1,8]{2,1,0:T(1,128)S(1)}, s32[1,1,8]{2,1,0:T(1,128)}, u32[]{:S(2)}) copy-start(s32[1,1,8]{2,1,0:T(1,128)} %lists_ref.1) | copy-start | bytes 100
  2.0 1.0 %copy-start = (bf16[1,2,1024,128]{3,2,1,0:T(8,128)(2,1)S(1)}, bf16[1,2,1024,128]{3,2,1,0:T(8,128)(2,1)}, u32[]{:S(2)}) copy-start(bf16[1,2,1024,128]{3,2,1,0:T(8,128)(2,1)} %strip_ref.1) | copy-start | bytes 1572868
  3.0 0.8 %copy-start.1 = (s32[1,1,8,2,1024]{4,3,2,1,0:T(2,128)S(1)}, s32[1,1,8,2,1024]{4,3,2,1,0:T(2,128)}, u32[]{:S(2)}) copy-start(s32[1,1,8,2,1024]{4,3,2,1,0:T(2,128)} %uv_ref.1) | copy-start | bytes 196612

commit v2 on v1

--- a/solution.py
+++ b/solution.py
@@ -18,6 +18,7 @@
 FACETS = 64
 LEN = 1024
 MESH = pl.DeviceIdType.MESH
+FAR = ((1, 2), (1, 1), (1, 3), (0, 2), (1, 0), (0, 1), (0, 3))
 F32 = jnp.float32
 BF16 = jnp.bfloat16
 I32 = jnp.int32
@@ -48,13 +49,18 @@
 
 def kernel(
     strip_ref,
+    offsets_hbm,
+    column_hbm,
+    row_hbm,
+    lists_hbm,
+    counts_hbm,
+    uv_ref,
+    out_ref,
     offsets_ref,
     column_ref,
     row_ref,
     lists_ref,
     counts_ref,
-    uv_ref,
-    out_ref,
     strip_v,
     uv_v,
     left_v,
@@ -97,21 +103,31 @@
     zp = z % 2
     q_me = x_hi * 2 + core
     g_me = q_me * 2 + zp
-    place = 8 * zp + zg
 
     loads = [
         pltpu.make_async_copy(strip_ref.at[0, 0], strip_v.at[:, pl.ds(0, W)], load_sem.at[0]),
         pltpu.make_async_copy(strip_ref.at[0, 1], strip_v.at[:, pl.ds(W, W)], load_sem.at[1]),
         pltpu.make_async_copy(uv_ref.at[0, 0], uv_v, load_sem.at[2]),
+        pltpu.make_async_copy(offsets_hbm, offsets_ref, load_sem.at[3]),
+        pltpu.make_async_copy(row_hbm, row_ref, load_sem.at[4]),
+        pltpu.make_async_copy(column_hbm, column_ref, load_sem.at[5]),
+        pltpu.make_async_copy(lists_hbm, lists_ref, load_sem.at[6]),
+        pltpu.make_async_copy(counts_hbm, counts_ref, load_sem.at[7]),
     ]
-    for load in loads:
-        load.start()
+    for n in (3, 4, 0, 1, 5, 6, 7, 2):
+        loads[n].start()
 
     barrier = pltpu.get_barrier_semaphore()
 
     def greet(f, c):
         pl.semaphore_signal(barrier, inc=1, device_id=(f, c), device_id_type=MESH)
 
+    for i in (4, 3, 5, 2, 6, 1, 7):
+        greet(facet_of(x_hi, (z + 2 * i) % 16, core), col)
+    for i in (3, 13):
+        greet(facet_of(x_hi, (z + i) % 16, core), col)
+    greet(facet_of(x_hi, (z + 2 * zp + 15) % 16, core), col)
+
     @pl.loop(1, 8)
     def _(i):
         greet(facet, (col + i) % 8)
@@ -119,18 +135,15 @@
     @pl.loop(1, 8)
     def _(i):
         greet(group_facet((g_me + i) % 8, zg), col)
-
-    @pl.loop(1, 16)
-    def _(i):
-        @pl.when((z + i) % 16 != 2 * zg + (1 - zp))
-        def _():
-            greet(facet_of(x_hi, (z + i) % 16, core), col)
 
     @pl.when(col != g_me)
     def _():
         @pl.loop(0, 8)
         def _(g):
             greet(group_facet(g, zg), g_me)
+
+    loads[3].wait()
+    loads[4].wait()
 
     row0 = row_ref[0]
     cells = offsets_ref[0, 0] + col * LEN + iota((8, LEN), 1)
@@ -155,7 +168,7 @@
     imag = both[:S, W:] - both[S:, :W]
     send1[...] = jnp.concatenate([real, imag], axis=1).astype(BF16).reshape(8, 32, 2 * W)
 
-    pl.semaphore_wait(barrier, 35)
+    pl.semaphore_wait(barrier, 31)
 
     def copy1(c):
         return pltpu.make_async_remote_copy(
@@ -169,12 +182,19 @@
             device_id=(facet, c), device_id_type=MESH,
         )
 
-    @pl.loop(1, 8)
-    def _(i):
-        copy1((col + i) % 8).start()
+    x_lo = col // 4
+    y = col % 4
+
+    def col_at(far):
+        return (x_lo + far[0]) % 2 * 4 + (y + far[1]) % 4
+
+    for far in FAR:
+        copy1(col_at(far)).start()
 
     recv1[pl.ds(col, 1)] = send1[pl.ds(col, 1)]
 
+    loads[6].wait()
+    loads[7].wait()
     lanes = iota((8, W), 0)
     ids = jnp.full((8, W), -1, I32)
     for j in range(CAP):
@@ -193,6 +213,7 @@
     def _(i):
         copy_s((g_me + i) % 8, g_me).start()
 
+    loads[5].wait()
     lane = iota((8, 2 * S), 1)
     sample = column_ref[0] + 256 * (32 * (lane // 64) + lane % 32)
     quarter = (NTOT // 4) * ((lane // 32) % 2)
@@ -242,9 +263,8 @@
     def _():
         copy2(col).start()
 
-    @pl.loop(1, 8)
-    def _(i):
-        copy2((col + i) % 8).start()
+    for far in FAR:
+        copy2(col_at(far)).start()
 
     loads[2].wait()
     for part in range(2):
@@ -303,7 +323,8 @@
 
     entry = iota((16, 2 * W), 1)
     diagonal = iota((16, 2 * W), 0) == entry % 16
-    entry = 16 * q_me + entry // 16
+    entry = entry // 16
+    entry = 16 * q_me + 8 * (entry // 2 % 2) + entry // 4 + 4 * (entry % 2)
 
     @pl.loop(0, 4)
     def _(q):
@@ -338,20 +359,19 @@
     for v in range(4):
         top = terms[0:16, W * v : W * v + W]
         low = terms[16:32, W * v : W * v + W]
-        send3[2 * v] = jnp.where(low_half, top, pltpu.roll(low, 64, 1)).astype(BF16)
-        send3[2 * v + 1] = jnp.where(low_half, pltpu.roll(top, 64, 1), low).astype(BF16)
-
-    def copy3(b, dst):
-        return pltpu.make_async_remote_copy(
-            src_ref=send3.at[b], dst_ref=recv3.at[dst], send_sem=s_3.at[b], recv_sem=r_3.at[dst],
-            device_id=(facet_of(x_hi, 2 * b + zp, core), col), device_id_type=MESH,
-        )
-
-    @pl.loop(1, 8)
-    def _(i):
+        send3[2 * v % 4, v // 2] = jnp.where(low_half, top, pltpu.roll(low, 64, 1)).astype(BF16)
+        send3[(2 * v + 1) % 4, v // 2] = jnp.where(low_half, pltpu.roll(top, 64, 1), low).astype(BF16)
+
+    def copy3(n, dst):
+        return pltpu.make_async_remote_copy(
+            src_ref=send3.at[n % 4], dst_ref=recv3.at[dst], send_sem=s_3.at[n], recv_sem=r_3.at[dst],
+            device_id=(facet_of(x_hi, 2 * n + zp, core), col), device_id_type=MESH,
+        )
+
+    for i in (4, 3, 5, 2, 6, 1, 7):
         copy3((zg + i) % 8, zg).start()
 
-    recv3[pl.ds(zg, 1)] = send3[pl.ds(zg, 1)]
+    recv3[pl.ds(zg, 1)] = send3[pl.ds(zg % 4, 1)]
 
     @pl.loop(1, 8)
     def _(i):
@@ -360,21 +380,28 @@
     total = recv3[0].astype(F32)
     for b in range(1, 8):
         total = total + recv3[b].astype(F32)
+    place = z % 8
     recv4[pl.ds(place, 1)] = total.astype(BF16)[None]
 
-    def copy4(n, dst):
-        return pltpu.make_async_remote_copy(
-            src_ref=recv4.at[place], dst_ref=recv4.at[dst], send_sem=s_4.at[n], recv_sem=r_4.at[dst],
-            device_id=(facet_of(x_hi, 2 * (n % 8) + n // 8, core), col), device_id_type=MESH,
-        )
-
-    @pl.loop(1, 16)
-    def _(i):
-        copy4((place + i) % 16, place).start()
-
-    @pl.loop(1, 16)
-    def _(i):
-        copy4((place + i) % 16, (place + i) % 16).wait_recv()
+    def copy4(i, dst):
+        return pltpu.make_async_remote_copy(
+            src_ref=recv4.at[place], dst_ref=recv4.at[dst], send_sem=s_4.at[dst], recv_sem=r_4.at[dst],
+            device_id=(facet_of(x_hi, (z + i) % 16, core), col), device_id_type=MESH,
+        )
+
+    def send4(i):
+        return pltpu.make_async_remote_copy(
+            src_ref=recv4.at[place], dst_ref=recv4.at[place],
+            send_sem=s_4.at[(place + i) % 8], recv_sem=r_4.at[place],
+            device_id=(facet_of(x_hi, (z + i) % 16, core), col), device_id_type=MESH,
+        )
+
+    for i in (4, 13, 3, 14, 2, 15, 1):
+        send4(i).start()
+
+    @pl.loop(1, 8)
+    def _(i):
+        copy4(i, (place + i) % 8).wait_recv()
 
     picks = jnp.dot(
         pick_v[...].reshape(4 * W, 2 * W), recv4[...].reshape(2 * W, W), preferred_element_type=F32
@@ -439,9 +466,9 @@
     def _():
         copy2(col).wait_send()
 
-    @pl.loop(1, 16)
-    def _(i):
-        copy4((place + i) % 16, place).wait_send()
+    @pl.loop(1, 8)
+    def _(i):
+        send4(i).wait_send()
 
     @pl.loop(1, 4)
     def _(i):
@@ -451,15 +478,19 @@
 def shards(
     facet_strips, facet_offsets, column_offsets, row_offsets, tile_lists, tile_counts, uv_index
 ):
-    smem = pl.BlockSpec(memory_space=pltpu.SMEM)
     anywhere = pl.BlockSpec(memory_space=pl.ANY)
     dma = pltpu.SemaphoreType.DMA
     return pl.pallas_call(
         kernel,
         out_shape=jax.ShapeDtypeStruct((1, 1, CAP, 2, VIS), F32),
-        in_specs=[anywhere, smem, smem, smem, smem, smem, anywhere],
+        in_specs=[anywhere] * 7,
         out_specs=pl.BlockSpec(memory_space=pltpu.VMEM),
         scratch_shapes=[
+            pltpu.SMEM((1, 2), I32),
+            pltpu.SMEM((1,), I32),
+            pltpu.SMEM((1,), I32),
+            pltpu.SMEM((1, 1, CAP), I32),
+            pltpu.SMEM((1, 1), I32),
             pltpu.VMEM((LEN, 2 * W), BF16),
             pltpu.VMEM((CAP, 2, VIS), I32),
             pltpu.VMEM((2 * S, LEN), BF16),
@@ -468,9 +499,9 @@
             pltpu.VMEM((32, 2 * W), BF16),
             pltpu.VMEM((8, 32, 2 * W), BF16),
             pltpu.VMEM((2 * W, 4 * S), BF16),
-            pltpu.VMEM((8, 16, W), BF16),
-            pltpu.VMEM((8, 16, W), BF16),
-            pltpu.VMEM((16, 16, W), BF16),
+            pltpu.VMEM((4, 2, 16, W), BF16),
+            pltpu.VMEM((8, 2, 16, W), BF16),
+            pltpu.VMEM((8, 2, 16, W), BF16),
             pltpu.VMEM((16, W), I32),
             pltpu.VMEM((8, 16, W), I32),
             pltpu.VMEM((4, W, 2 * W), BF16),
@@ -479,22 +510,22 @@
             pltpu.VMEM((2, 5, 2, CAP, VIS), F32),
             pltpu.VMEM((2, CAP, TILE, VIS), F32),
             pltpu.VMEM((CAP * 64, 2 * VIS), BF16),
-            dma((3,)),
-            dma((8,)),
-            dma((8,)),
-            dma((8,)),
-            dma((8,)),
-            dma((8,)),
-            dma((8,)),
-            dma((8,)),
-            dma((8,)),
-            dma((16,)),
-            dma((16,)),
+            dma((8,)),
+            dma((8,)),
+            dma((8,)),
+            dma((8,)),
+            dma((8,)),
+            dma((8,)),
+            dma((8,)),
+            dma((8,)),
+            dma((8,)),
+            dma((8,)),
+            dma((8,)),
             dma((4,)),
             dma((4,)),
         ],
         compiler_params=pltpu.CompilerParams(
-            collective_id=0, has_side_effects=True, vmem_limit_bytes=48 * 1024 * 1024
+            collective_id=0, has_side_effects=True, vmem_limit_bytes=63 * 1024 * 1024
         ),
     )(facet_strips, facet_offsets, column_offsets, row_offsets, tile_lists, tile_counts, uv_index)
 

time: 55 us -> 48.3 us (0.88)
  Pallas kernels: 50.3 us -> 44.7 us
  local copies, waits for them, and re-layouts: 2.51 us -> 1.47 us
    pallas_call x1, Pallas kernels: 50.3 us -> 44.7 us  [shards(): pl.pallas_call(kernel, out_shape=jax.ShapeDtypeStruct((1, 1, CAP, 2, VIS)...]
    unnamed x9 -> x1, local copies, waits for them, and re-layouts: 2.51 us -> 1.47 us
where the time goes in v2:
time: 48.3 us; the launch traced here: 48.1 us
  Pallas kernels  44.7 us (93%)
  between operations  1.95 us (4%)
  local copies, waits for them, and re-layouts  1.47 us (3%)
    pallas_call x1, Pallas kernels, shards(): pl.pallas_call(kernel, out_shape=jax.ShapeDtypeStruct((1, 1, CAP, 2, VIS)...  44.7 us
    unnamed x1, local copies, waits for them, and re-layouts  1.47 us

profile of v2, /device:TPU:1, one launch (start us, length us, event | category | flops | bytes accessed | tf_op | source)
XLA Modules:
  0.0 48.1 jit_solution(2515291548689189572)
XLA Ops:
  1.9 44.7 %shard_map.73 = f32[1,1,8,2,1024]{4,3,2,1,0:T(2,128)} custom-call(bf16[1,2,1024,128]{3,2,1,0:T(8,128)(2,1)} %strip_ref.1, s32[1,2]{1,0:T(1,128)} %offsets_hbm.1, s32[1]{0:T(128)S(6)} %copy.9.column_hbm, s32[1]{0:T(128)S(6)} %copy.10.row_hbm, s32[1,1,8]{2,1,0:T(1,128)} %lists_hbm.1, s32[1,1]{1,0:T(1,128)S(6)} %copy.11.counts_hbm, s32[1,1,8,2,1024]{4,3,2,1,0:T(2,128)} %uv_ref.1), custom_call_target="tpu_custom_call" | custom-call | tf_op jit(solution)/shard_map/pallas_call | solution.py:483
  46.6 1.5 %copy.12 = f32[1,1,8,2,1024]{4,3,2,1,0:T(2,128)} copy(f32[1,1,8,2,1024]{4,3,2,1,0:T(2,128)} %shard_map.73) | data formatting | bytes 131072

commit v3 on v2

--- a/solution.py
+++ b/solution.py
@@ -18,6 +18,9 @@
 FACETS = 64
 LEN = 1024
 MESH = pl.DeviceIdType.MESH
+DEAL = 0
+ORDER2 = ((0, 2), (0, 1), (0, 3), (1, 2), (0, 0), (1, 1), (1, 3), (1, 0))
+AROUND = (4, -3, 3, -2, 2, -1, 1, 0)
 FAR = ((1, 2), (1, 1), (1, 3), (0, 2), (1, 0), (0, 1), (0, 3))
 F32 = jnp.float32
 BF16 = jnp.bfloat16
@@ -74,6 +77,8 @@
     recv4,
     small_v,
     recv_s,
+    ids_v,
+    recv_i,
     pick_v,
     send5,
     recv5,
@@ -83,6 +88,8 @@
     load_sem,
     s_s,
     r_s,
+    s_i,
+    r_i,
     s_1,
     r_1,
     s_2,
@@ -103,6 +110,16 @@
     zp = z % 2
     q_me = x_hi * 2 + core
     g_me = q_me * 2 + zp
+    x_lo = col // 4
+    y = col % 4
+
+    def block_of(c, x):
+        return (c // 4 + x + DEAL) % 2 * 4 + c % 4
+
+    def col_of(block, x):
+        return (block // 4 + x + DEAL) % 2 * 4 + block % 4
+
+    target = block_of(col, x_hi)
 
     loads = [
         pltpu.make_async_copy(strip_ref.at[0, 0], strip_v.at[:, pl.ds(0, W)], load_sem.at[0]),
@@ -127,6 +144,8 @@
     for i in (3, 13):
         greet(facet_of(x_hi, (z + i) % 16, core), col)
     greet(facet_of(x_hi, (z + 2 * zp + 15) % 16, core), col)
+    for i in (-4, 3, -3, 2, -2, 2 * zp - 1):
+        greet(facet_of(1 - x_hi, (z + 16 + i) % 16, core), col)
 
     @pl.loop(1, 8)
     def _(i):
@@ -136,11 +155,13 @@
     def _(i):
         greet(group_facet((g_me + i) % 8, zg), col)
 
-    @pl.when(col != g_me)
-    def _():
-        @pl.loop(0, 8)
-        def _(g):
-            greet(group_facet(g, zg), g_me)
+    @pl.loop(0, 8)
+    def _(g):
+        source = col_of(g_me, g // 4)
+
+        @pl.when(source != col)
+        def _():
+            greet(group_facet(g, zg), source)
 
     loads[3].wait()
     loads[4].wait()
@@ -168,22 +189,19 @@
     imag = both[:S, W:] - both[S:, :W]
     send1[...] = jnp.concatenate([real, imag], axis=1).astype(BF16).reshape(8, 32, 2 * W)
 
-    pl.semaphore_wait(barrier, 31)
+    pl.semaphore_wait(barrier, 37)
 
     def copy1(c):
         return pltpu.make_async_remote_copy(
-            src_ref=send1.at[c], dst_ref=recv1.at[col], send_sem=s_1.at[c], recv_sem=r_1.at[col],
+            src_ref=send1.at[block_of(c, x_hi)], dst_ref=recv1.at[col], send_sem=s_1.at[c], recv_sem=r_1.at[col],
             device_id=(facet, c), device_id_type=MESH,
         )
 
     def from1(c):
         return pltpu.make_async_remote_copy(
-            src_ref=send1.at[c], dst_ref=recv1.at[c], send_sem=s_1.at[c], recv_sem=r_1.at[c],
+            src_ref=send1.at[block_of(c, x_hi)], dst_ref=recv1.at[c], send_sem=s_1.at[c], recv_sem=r_1.at[c],
             device_id=(facet, c), device_id_type=MESH,
         )
-
-    x_lo = col // 4
-    y = col % 4
 
     def col_at(far):
         return (x_lo + far[0]) % 2 * 4 + (y + far[1]) % 4
@@ -191,7 +209,7 @@
     for far in FAR:
         copy1(col_at(far)).start()
 
-    recv1[pl.ds(col, 1)] = send1[pl.ds(col, 1)]
+    recv1[pl.ds(col, 1)] = send1[pl.ds(target, 1)]
 
     loads[6].wait()
     loads[7].wait()
@@ -199,8 +217,8 @@
     ids = jnp.full((8, W), -1, I32)
     for j in range(CAP):
         ids = jnp.where((lanes == j) & (j < counts_ref[0, 0]), lists_ref[0, 0, j], ids)
-    small_v[0:8, :] = ids
-    small_v[8:16, :] = jnp.full((8, W), offsets_ref[0, 1], I32)
+    ids_v[...] = ids
+    small_v[...] = jnp.full((8, W), offsets_ref[0, 1], I32)
     recv_s[pl.ds(g_me, 1)] = small_v[...][None]
 
     def copy_s(g, dst):
@@ -208,6 +226,12 @@
             src_ref=small_v, dst_ref=recv_s.at[dst], send_sem=s_s.at[g], recv_sem=r_s.at[dst],
             device_id=(group_facet(g, zg), col), device_id_type=MESH,
         )
+
+    copy_i = pltpu.make_async_remote_copy(
+        src_ref=ids_v, dst_ref=recv_i, send_sem=s_i, recv_sem=r_i,
+        device_id=(facet_of(x_hi, z, 1 - core), col), device_id_type=MESH,
+    )
+    copy_i.start()
 
     @pl.loop(1, 8)
     def _(i):
@@ -246,25 +270,25 @@
     def copy2(c):
         return pltpu.make_async_remote_copy(
             src_ref=block2, dst_ref=recv2.at[g_me], send_sem=s_2.at[c], recv_sem=r_2.at[g_me],
-            device_id=(group_facet(col, zg), c), device_id_type=MESH,
+            device_id=(group_facet(target, zg), c), device_id_type=MESH,
         )
 
     def from2(g):
         return pltpu.make_async_remote_copy(
             src_ref=block2, dst_ref=recv2.at[g], send_sem=s_2.at[g], recv_sem=r_2.at[g],
-            device_id=(group_facet(g, zg), g_me), device_id_type=MESH,
-        )
-
-    @pl.when(col == g_me)
+            device_id=(group_facet(g, zg), col_of(g_me, g // 4)), device_id_type=MESH,
+        )
+
+    for x, dy in ORDER2:
+        c = 4 * x + (y + dy) % 4
+
+        @pl.when((target != g_me) | (c != col))
+        def _():
+            copy2(c).start()
+
+    @pl.when(target == g_me)
     def _():
         recv2[pl.ds(g_me, 1)] = block2[...][None]
-
-    @pl.when(col != g_me)
-    def _():
-        copy2(col).start()
-
-    for far in FAR:
-        copy2(col_at(far)).start()
 
     loads[2].wait()
     for part in range(2):
@@ -315,35 +339,28 @@
 
     across = jnp.zeros((8, W), I32)
     for g in range(8):
-        across = jnp.where(lanes == g, recv_s[g, 8:16, :], across)
+        across = jnp.where(lanes == g, recv_s[g], across)
     across = jnp.concatenate([across] * 4, axis=1)
     turn = unit(across * sample)
     norm = 1.0 / math.sqrt(W * FACETS)
     turn = (turn[0] * norm, turn[1] * norm)
 
-    entry = iota((16, 2 * W), 1)
-    diagonal = iota((16, 2 * W), 0) == entry % 16
+    copy_i.wait_recv()
+    entry = iota((16, 4 * W), 1)
+    diagonal = iota((16, 4 * W), 0) == entry % 16
     entry = entry // 16
-    entry = 16 * q_me + 8 * (entry // 2 % 2) + entry // 4 + 4 * (entry % 2)
-
-    @pl.loop(0, 4)
-    def _(q):
+    at_place = entry // 2 % 8
+    entry = 32 * (entry // 16) + 16 * core + 8 * (at_place % 2) + at_place // 2 + 4 * (entry % 2)
+    for n, wanted_ref in enumerate((ids_v, recv_i)):
         for j in range(CAP):
-            wanted = recv_s[2 * q + zp, j : j + 1, :]
-            wanted = jnp.broadcast_to(jnp.concatenate([wanted, wanted], axis=1), (16, 2 * W))
-            pick = jnp.where((wanted == entry) & diagonal, 1.0, 0.0)
-            pick_v[q, 16 * j : 16 * j + 16, :] = pick.astype(BF16)
-
-    @pl.when(col == g_me)
-    def _():
-        @pl.loop(1, 8)
-        def _(i):
-            from2((g_me + i) % 8).wait_recv()
-
-    @pl.when(col != g_me)
-    def _():
-        @pl.loop(0, 8)
-        def _(g):
+            wanted = jnp.concatenate([wanted_ref[j : j + 1, :]] * 4, axis=1)
+            pick = jnp.where((jnp.broadcast_to(wanted, entry.shape) == entry) & diagonal, 1.0, 0.0)
+            pick_v[W * n + 16 * j : W * n + 16 * j + 16, :] = pick.astype(BF16)
+
+    @pl.loop(0, 8)
+    def _(g):
+        @pl.when((target != g_me) | (g != g_me))
+        def _():
             from2(g).wait_recv()
 
     grid = jnp.dot(
@@ -381,52 +398,35 @@
     for b in range(1, 8):
         total = total + recv3[b].astype(F32)
     place = z % 8
-    recv4[pl.ds(place, 1)] = total.astype(BF16)[None]
-
-    def copy4(i, dst):
-        return pltpu.make_async_remote_copy(
-            src_ref=recv4.at[place], dst_ref=recv4.at[dst], send_sem=s_4.at[dst], recv_sem=r_4.at[dst],
-            device_id=(facet_of(x_hi, (z + i) % 16, core), col), device_id_type=MESH,
-        )
-
-    def send4(i):
-        return pltpu.make_async_remote_copy(
-            src_ref=recv4.at[place], dst_ref=recv4.at[place],
-            send_sem=s_4.at[(place + i) % 8], recv_sem=r_4.at[place],
-            device_id=(facet_of(x_hi, (z + i) % 16, core), col), device_id_type=MESH,
-        )
-
-    for i in (4, 13, 3, 14, 2, 15, 1):
-        send4(i).start()
-
-    @pl.loop(1, 8)
-    def _(i):
-        copy4(i, (place + i) % 8).wait_recv()
-
-    picks = jnp.dot(
-        pick_v[...].reshape(4 * W, 2 * W), recv4[...].reshape(2 * W, W), preferred_element_type=F32
+    mine = 8 * x_hi + place
+    recv4[pl.ds(mine, 1)] = total.astype(BF16)[None]
+
+    def copy4(x, i, dst):
+        there = 8 * x + (place + i) % 8
+        return pltpu.make_async_remote_copy(
+            src_ref=recv4.at[mine], dst_ref=recv4.at[dst], send_sem=s_4.at[there], recv_sem=r_4.at[dst],
+            device_id=(facet_of(x, (z + i) % 16, core), col), device_id_type=MESH,
+        )
+
+    for i in AROUND:
+        copy4(1 - x_hi, i + 16, mine).start()
+    for i in AROUND[:-1]:
+        copy4(x_hi, i + 16, mine).start()
+
+    @pl.loop(1, 16)
+    def _(i):
+        n = (mine + i) % 16
+        copy4(n // 8, n % 8 - place + 16, n).wait_recv()
+
+    picks = jnp.dot(pick_v[...], recv4[...].reshape(4 * W, W), preferred_element_type=F32)
+    send5[...] = picks.astype(BF16).reshape(2, W, W)
+    copy5 = pltpu.make_async_remote_copy(
+        src_ref=send5.at[1], dst_ref=recv5, send_sem=s_5, recv_sem=r_5,
+        device_id=(facet_of(x_hi, z, 1 - core), col), device_id_type=MESH,
     )
-    send5[...] = picks.astype(BF16).reshape(4, W, W)
-
-    def copy5(q, dst):
-        return pltpu.make_async_remote_copy(
-            src_ref=send5.at[q], dst_ref=recv5.at[dst], send_sem=s_5.at[q], recv_sem=r_5.at[dst],
-            device_id=(facet_of(q // 2, z, q % 2), col), device_id_type=MESH,
-        )
-
-    @pl.loop(1, 4)
-    def _(i):
-        copy5((q_me + i) % 4, q_me).start()
-
-    recv5[pl.ds(q_me, 1)] = send5[pl.ds(q_me, 1)]
-
-    @pl.loop(1, 4)
-    def _(i):
-        copy5((q_me + i) % 4, (q_me + i) % 4).wait_recv()
-
-    chosen = recv5[0].astype(F32)
-    for q in range(1, 4):
-        chosen = chosen + recv5[q].astype(F32)
+    copy5.start()
+    copy5.wait_recv()
+    chosen = send5[0].astype(F32) + recv5[...].astype(F32)
 
     for h in range(2):
         rows = []
@@ -459,20 +459,22 @@
     def _(i):
         copy1((col + i) % 8).wait_send()
         copy_s((g_me + i) % 8, g_me).wait_send()
-        copy2((col + i) % 8).wait_send()
         copy3((zg + i) % 8, zg).wait_send()
 
-    @pl.when(col != g_me)
-    def _():
-        copy2(col).wait_send()
-
-    @pl.loop(1, 8)
-    def _(i):
-        send4(i).wait_send()
-
-    @pl.loop(1, 4)
-    def _(i):
-        copy5((q_me + i) % 4, q_me).wait_send()
+    copy_i.wait_send()
+
+    @pl.loop(0, 8)
+    def _(c):
+        @pl.when((target != g_me) | (c != col))
+        def _():
+            copy2(c).wait_send()
+
+    @pl.loop(1, 16)
+    def _(i):
+        n = (mine + i) % 16
+        copy4(n // 8, n % 8 - place + 16, mine).wait_send()
+
+    copy5.wait_send()
 
 
 def shards(
@@ -501,31 +503,35 @@
             pltpu.VMEM((2 * W, 4 * S), BF16),
             pltpu.VMEM((4, 2, 16, W), BF16),
             pltpu.VMEM((8, 2, 16, W), BF16),
-            pltpu.VMEM((8, 2, 16, W), BF16),
-            pltpu.VMEM((16, W), I32),
-            pltpu.VMEM((8, 16, W), I32),
-            pltpu.VMEM((4, W, 2 * W), BF16),
-            pltpu.VMEM((4, W, W), BF16),
-            pltpu.VMEM((4, W, W), BF16),
+            pltpu.VMEM((16, 2, 16, W), BF16),
+            pltpu.VMEM((8, W), I32),
+            pltpu.VMEM((8, 8, W), I32),
+            pltpu.VMEM((8, W), I32),
+            pltpu.VMEM((8, W), I32),
+            pltpu.VMEM((2 * W, 4 * W), BF16),
+            pltpu.VMEM((2, W, W), BF16),
+            pltpu.VMEM((W, W), BF16),
             pltpu.VMEM((2, 5, 2, CAP, VIS), F32),
             pltpu.VMEM((2, CAP, TILE, VIS), F32),
             pltpu.VMEM((CAP * 64, 2 * VIS), BF16),
             dma((8,)),
             dma((8,)),
             dma((8,)),
-            dma((8,)),
-            dma((8,)),
-            dma((8,)),
-            dma((8,)),
-            dma((8,)),
-            dma((8,)),
-            dma((8,)),
-            dma((8,)),
-            dma((4,)),
-            dma((4,)),
+            dma,
+            dma,
+            dma((8,)),
+            dma((8,)),
+            dma((8,)),
+            dma((8,)),
+            dma((8,)),
+            dma((8,)),
+            dma((16,)),
+            dma((16,)),
+            dma,
+            dma,
         ],
         compiler_params=pltpu.CompilerParams(
-            collective_id=0, has_side_effects=True, vmem_limit_bytes=63 * 1024 * 1024
+            collective_id=0, has_side_effects=True, vmem_limit_bytes=55104 * 1024
         ),
     )(facet_strips, facet_offsets, column_offsets, row_offsets, tile_lists, tile_counts, uv_index)
 

time: 48.3 us -> 46 us (0.952)
  Pallas kernels: 44.7 us -> 43.2 us
  local copies, waits for them, and re-layouts: 1.47 us -> 0.64 us
    pallas_call x1, Pallas kernels: 44.7 us -> 43.2 us  [shards(): pl.pallas_call(kernel, out_shape=jax.ShapeDtypeStruct((1, 1, CAP, 2, VIS)...]
    unnamed x1 -> x5, local copies, waits for them, and re-layouts: 1.47 us -> 0.64 us
where the time goes in v3:
time: 46 us; the launch traced here: 45.8 us
  Pallas kernels  43.2 us (94%)
  between operations  2 us (4%)
  local copies, waits for them, and re-layouts  0.64 us (1%)
    pallas_call x1, Pallas kernels, shards(): pl.pallas_call(kernel, out_shape=jax.ShapeDtypeStruct((1, 1, CAP, 2, VIS)...  43.2 us

profile of v3, /device:TPU:1, one launch (start us, length us, event | category | flops | bytes accessed | tf_op | source)
XLA Modules:
  0.0 45.8 jit_solution(2462742533213964517)
XLA Ops:
  1.3 0.0 copy-start
  1.3 0.0 copy-start.1
  2.0 0.0 copy-done
  2.0 0.0 copy-done.1
  2.0 43.2 %shard_map.73 = f32[1,1,8,2,1024]{4,3,2,1,0:T(2,128)S(1)} custom-call(bf16[1,2,1024,128]{3,2,1,0:T(8,128)(2,1)} %strip_ref.1, s32[1,2]{1,0:T(1,128)S(1)} %copy-done, s32[1]{0:T(128)S(6)} %copy.9.column_hbm, s32[1]{0:T(128)S(6)} %copy.10.row_hbm, s32[1,1,8]{2,1,0:T(1,128)S(1)} %copy-done.1, s32[1,1]{1,0:T(1,128)S(6)} %copy.11.counts_hbm, ...), custom_call_target="tpu_custom_call" | custom-call | tf_op jit(solution)/shard_map/pallas_call | solution.py:485
  45.2 0.6 %copy.12 = f32[1,1,8,2,1024]{4,3,2,1,0:T(2,128)} copy(f32[1,1,8,2,1024]{4,3,2,1,0:T(2,128)S(1)} %shard_map.73) | data formatting | bytes 131072
Async XLA Ops:
  1.3 0.7 %copy-start = (s32[1,2]{1,0:T(1,128)S(1)}, s32[1,2]{1,0:T(1,128)}, u32[]{:S(2)}) copy-start(s32[1,2]{1,0:T(1,128)} %offsets_hbm.1) | copy-start | bytes 28
  1.3 0.7 %copy-start.1 = (s32[1,1,8]{2,1,0:T(1,128)S(1)}, s32[1,1,8]{2,1,0:T(1,128)}, u32[]{:S(2)}) copy-start(s32[1,1,8]{2,1,0:T(1,128)} %lists_hbm.1) | copy-start | bytes 100

commit v4 on v3

--- a/solution.py
+++ b/solution.py
@@ -77,6 +77,7 @@
     recv4,
     small_v,
     recv_s,
+    turn_v,
     ids_v,
     recv_i,
     pick_v,
@@ -100,6 +101,9 @@
     r_4,
     s_5,
     r_5,
+    word_2,
+    word_3,
+    word_4,
 ):
     facet = lax.axis_index("facet")
     col = lax.axis_index("col")
@@ -139,13 +143,11 @@
     def greet(f, c):
         pl.semaphore_signal(barrier, inc=1, device_id=(f, c), device_id_type=MESH)
 
-    for i in (4, 3, 5, 2, 6, 1, 7):
-        greet(facet_of(x_hi, (z + 2 * i) % 16, core), col)
-    for i in (3, 13):
-        greet(facet_of(x_hi, (z + i) % 16, core), col)
-    greet(facet_of(x_hi, (z + 2 * zp + 15) % 16, core), col)
-    for i in (-4, 3, -3, 2, -2, 2 * zp - 1):
-        greet(facet_of(1 - x_hi, (z + 16 + i) % 16, core), col)
+    def along(i):
+        return facet_of(x_hi, (z + i + 16) % 16, core)
+
+    for i in (4, -4, 3, -3, 2, -2, 2 * zp - 1):
+        greet(along(i), col)
 
     @pl.loop(1, 8)
     def _(i):
@@ -154,14 +156,6 @@
     @pl.loop(1, 8)
     def _(i):
         greet(group_facet((g_me + i) % 8, zg), col)
-
-    @pl.loop(0, 8)
-    def _(g):
-        source = col_of(g_me, g // 4)
-
-        @pl.when(source != col)
-        def _():
-            greet(group_facet(g, zg), source)
 
     loads[3].wait()
     loads[4].wait()
@@ -189,7 +183,7 @@
     imag = both[:S, W:] - both[S:, :W]
     send1[...] = jnp.concatenate([real, imag], axis=1).astype(BF16).reshape(8, 32, 2 * W)
 
-    pl.semaphore_wait(barrier, 37)
+    pl.semaphore_wait(barrier, 21)
 
     def copy1(c):
         return pltpu.make_async_remote_copy(
@@ -209,7 +203,18 @@
     for far in FAR:
         copy1(col_at(far)).start()
 
-    recv1[pl.ds(col, 1)] = send1[pl.ds(target, 1)]
+    def tell(sem, f):
+        pl.semaphore_signal(sem, inc=1, device_id=(f, col), device_id_type=MESH)
+
+    for g in range(8):
+
+        @pl.when((block_of(col, g // 4) == g_me) & (g != g_me))
+        def _():
+            tell(word_2, group_facet(g, zg))
+
+    tell(word_3, along(4))
+    tell(word_3, along(-4))
+    tell(word_4, facet_of(1 - x_hi, z, core))
 
     loads[6].wait()
     loads[7].wait()
@@ -258,14 +263,12 @@
 
     lax.fori_loop(0, 8, right_body, base_r)
 
-    @pl.loop(1, 8)
-    def _(i):
-        from1((col + i) % 8).wait_recv()
-
-    total = recv1[0].astype(F32)
-    for c in range(1, 8):
-        total = total + recv1[c].astype(F32)
-    block2[...] = total.astype(BF16)
+    total = send1[pl.ds(target, 1)].astype(F32)
+    for far in FAR[::-1]:
+        c = col_at(far)
+        from1(c).wait_recv()
+        total = total + recv1[pl.ds(c, 1)].astype(F32)
+    block2[...] = total[0].astype(BF16)
 
     def copy2(c):
         return pltpu.make_async_remote_copy(
@@ -278,6 +281,10 @@
             src_ref=block2, dst_ref=recv2.at[g], send_sem=s_2.at[g], recv_sem=r_2.at[g],
             device_id=(group_facet(g, zg), col_of(g_me, g // 4)), device_id_type=MESH,
         )
+
+    @pl.when(target != g_me)
+    def _():
+        pl.semaphore_wait(word_2, 1)
 
     for x, dy in ORDER2:
         c = 4 * x + (y + dy) % 4
@@ -343,34 +350,47 @@
     across = jnp.concatenate([across] * 4, axis=1)
     turn = unit(across * sample)
     norm = 1.0 / math.sqrt(W * FACETS)
-    turn = (turn[0] * norm, turn[1] * norm)
+    turn_v[0] = turn[0] * norm
+    turn_v[1] = turn[1] * norm
 
     copy_i.wait_recv()
     entry = iota((16, 4 * W), 1)
     diagonal = iota((16, 4 * W), 0) == entry % 16
     entry = entry // 16
     at_place = entry // 2 % 8
-    entry = 32 * (entry // 16) + 16 * core + 8 * (at_place % 2) + at_place // 2 + 4 * (entry % 2)
+    entry = 32 * ((entry // 16 + x_hi) % 2) + 16 * core + 8 * (at_place % 2) + at_place // 2 + 4 * (entry % 2)
     for n, wanted_ref in enumerate((ids_v, recv_i)):
         for j in range(CAP):
             wanted = jnp.concatenate([wanted_ref[j : j + 1, :]] * 4, axis=1)
             pick = jnp.where((jnp.broadcast_to(wanted, entry.shape) == entry) & diagonal, 1.0, 0.0)
-            pick_v[W * n + 16 * j : W * n + 16 * j + 16, :] = pick.astype(BF16)
-
-    @pl.loop(0, 8)
-    def _(g):
-        @pl.when((target != g_me) | (g != g_me))
-        def _():
-            from2(g).wait_recv()
-
-    grid = jnp.dot(
-        recv2[...].reshape(8 * 32, 2 * W), table_v[...], preferred_element_type=F32
-    )
+            at = 2 * 64 * (j // 4) + 64 * n + 16 * (j % 4)
+            pick_v[at : at + 16, :] = pick.astype(BF16)
+
+    @pl.loop(1, 8)
+    def _(i):
+        copy1((col + i) % 8).wait_send()
+        copy_s((g_me + i) % 8, g_me).wait_send()
+
+    copy_i.wait_send()
+
     terms = None
-    for g in range(8):
-        rows = grid[32 * g : 32 * g + 32]
-        term = rows[:, : 2 * S] * turn[0][g : g + 1] + rows[:, 2 * S :] * turn[1][g : g + 1]
-        terms = term if terms is None else terms + term
+    for x in range(2):
+        first = (x_hi + x) % 2 * 4
+
+        @pl.loop(first, first + 4)
+        def _(g):
+            @pl.when((target != g_me) | (g != g_me))
+            def _():
+                from2(g).wait_recv()
+
+        grid = jnp.dot(
+            recv2[pl.ds(first, 4)].reshape(4 * 32, 2 * W), table_v[...], preferred_element_type=F32
+        )
+        for g in range(4):
+            rows = grid[32 * g : 32 * g + 32]
+            re, im = (turn_v[h, pl.ds(first + g, 1), :] for h in range(2))
+            term = rows[:, : 2 * S] * re + rows[:, 2 * S :] * im
+            terms = term if terms is None else terms + term
 
     low_half = iota((16, W), 1) < 64
     for v in range(4):
@@ -385,53 +405,82 @@
             device_id=(facet_of(x_hi, 2 * n + zp, core), col), device_id_type=MESH,
         )
 
+    pl.semaphore_wait(word_3, 2)
     for i in (4, 3, 5, 2, 6, 1, 7):
         copy3((zg + i) % 8, zg).start()
 
-    recv3[pl.ds(zg, 1)] = send3[pl.ds(zg % 4, 1)]
-
-    @pl.loop(1, 8)
-    def _(i):
-        copy3((zg + i) % 8, (zg + i) % 8).wait_recv()
-
-    total = recv3[0].astype(F32)
-    for b in range(1, 8):
-        total = total + recv3[b].astype(F32)
+    total = send3[pl.ds(zg % 4, 1)].astype(F32)
+    for i in (1, 7, 2, 6, 3, 5, 4):
+        n = (zg + i) % 8
+        copy3(n, n).wait_recv()
+        total = total + recv3[pl.ds(n, 1)].astype(F32)
+
     place = z % 8
-    mine = 8 * x_hi + place
-    recv4[pl.ds(mine, 1)] = total.astype(BF16)[None]
+    recv4[pl.ds(place, 1)] = total.astype(BF16)
 
     def copy4(x, i, dst):
         there = 8 * x + (place + i) % 8
         return pltpu.make_async_remote_copy(
-            src_ref=recv4.at[mine], dst_ref=recv4.at[dst], send_sem=s_4.at[there], recv_sem=r_4.at[dst],
-            device_id=(facet_of(x, (z + i) % 16, core), col), device_id_type=MESH,
-        )
-
+            src_ref=recv4.at[place], dst_ref=recv4.at[dst], send_sem=s_4.at[there], recv_sem=r_4.at[dst],
+            device_id=(facet_of((x_hi + x) % 2, (z + i) % 16, core), col), device_id_type=MESH,
+        )
+
+    pl.semaphore_wait(word_4, 1)
     for i in AROUND:
-        copy4(1 - x_hi, i + 16, mine).start()
+        copy4(1, i + 16, 8 + place).start()
     for i in AROUND[:-1]:
-        copy4(x_hi, i + 16, mine).start()
-
-    @pl.loop(1, 16)
-    def _(i):
-        n = (mine + i) % 16
-        copy4(n // 8, n % 8 - place + 16, n).wait_recv()
-
-    picks = jnp.dot(pick_v[...], recv4[...].reshape(4 * W, W), preferred_element_type=F32)
-    send5[...] = picks.astype(BF16).reshape(2, W, W)
-    copy5 = pltpu.make_async_remote_copy(
-        src_ref=send5.at[1], dst_ref=recv5, send_sem=s_5, recv_sem=r_5,
-        device_id=(facet_of(x_hi, z, 1 - core), col), device_id_type=MESH,
+        copy4(0, i + 16, place).start()
+
+    @pl.loop(0, 8)
+    def _(c):
+        @pl.when((target != g_me) | (c != col))
+        def _():
+            copy2(c).wait_send()
+
+    @pl.loop(1, 8)
+    def _(i):
+        n = (place + i) % 8
+        copy4(0, i, n).wait_recv()
+
+    half = 2 * W
+    near = jnp.dot(
+        pick_v[:, :half], recv4[0:8].reshape(half, W), preferred_element_type=F32
     )
-    copy5.start()
-    copy5.wait_recv()
-    chosen = send5[0].astype(F32) + recv5[...].astype(F32)
+
+    @pl.loop(0, 8)
+    def _(i):
+        n = (place + i) % 8
+        copy4(1, i, 8 + n).wait_recv()
+
+    def copy5(h):
+        return pltpu.make_async_remote_copy(
+            src_ref=send5.at[h, 1], dst_ref=recv5.at[h], send_sem=s_5.at[h], recv_sem=r_5.at[h],
+            device_id=(facet_of(x_hi, z, 1 - core), col), device_id_type=MESH,
+        )
 
     for h in range(2):
+        rows = slice(W * h, W * h + W)
+        picks = near[rows] + jnp.dot(
+            pick_v[rows, half:], recv4[8:16].reshape(half, W), preferred_element_type=F32
+        )
+        send5[h] = picks.astype(BF16).reshape(2, 64, W)
+        copy5(h).start()
+
+    @pl.loop(1, 8)
+    def _(i):
+        copy3((zg + i) % 8, zg).wait_send()
+        copy4(0, i, place).wait_send()
+
+    @pl.loop(0, 8)
+    def _(i):
+        copy4(1, i, 8 + place).wait_send()
+
+    for h in range(2):
+        copy5(h).wait_recv()
+        chosen = send5[h, 0].astype(F32) + recv5[h].astype(F32)
         rows = []
         for i in range(4):
-            tile = chosen[64 * h + 16 * i : 64 * h + 16 * i + 16]
+            tile = chosen[16 * i : 16 * i + 16]
             other = pltpu.roll(tile, 64, 1)
             if i % 2 == 0:
                 top, low = jnp.where(low_half, tile, 0.0), jnp.where(low_half, other, 0.0)
@@ -455,26 +504,8 @@
                         vis[part], axis=0, keepdims=True
                     )
 
-    @pl.loop(1, 8)
-    def _(i):
-        copy1((col + i) % 8).wait_send()
-        copy_s((g_me + i) % 8, g_me).wait_send()
-        copy3((zg + i) % 8, zg).wait_send()
-
-    copy_i.wait_send()
-
-    @pl.loop(0, 8)
-    def _(c):
-        @pl.when((target != g_me) | (c != col))
-        def _():
-            copy2(c).wait_send()
-
-    @pl.loop(1, 16)
-    def _(i):
-        n = (mine + i) % 16
-        copy4(n // 8, n % 8 - place + 16, mine).wait_send()
-
-    copy5.wait_send()
+    copy5(0).wait_send()
+    copy5(1).wait_send()
 
 
 def shards(
@@ -506,11 +537,12 @@
             pltpu.VMEM((16, 2, 16, W), BF16),
             pltpu.VMEM((8, W), I32),
             pltpu.VMEM((8, 8, W), I32),
+            pltpu.VMEM((2, 8, 2 * S), F32),
             pltpu.VMEM((8, W), I32),
             pltpu.VMEM((8, W), I32),
             pltpu.VMEM((2 * W, 4 * W), BF16),
-            pltpu.VMEM((2, W, W), BF16),
-            pltpu.VMEM((W, W), BF16),
+            pltpu.VMEM((2, 2, 64, W), BF16),
+            pltpu.VMEM((2, 64, W), BF16),
             pltpu.VMEM((2, 5, 2, CAP, VIS), F32),
             pltpu.VMEM((2, CAP, TILE, VIS), F32),
             pltpu.VMEM((CAP * 64, 2 * VIS), BF16),
@@ -527,8 +559,11 @@
             dma((8,)),
             dma((16,)),
             dma((16,)),
-            dma,
-            dma,
+            dma((2,)),
+            dma((2,)),
+            pltpu.SemaphoreType.REGULAR,
+            pltpu.SemaphoreType.REGULAR,
+            pltpu.SemaphoreType.REGULAR,
         ],
         compiler_params=pltpu.CompilerParams(
             collective_id=0, has_side_effects=True, vmem_limit_bytes=55104 * 1024

time: 46 us -> 43.4 us (0.943)
  Pallas kernels: 43.2 us -> 40.6 us
    pallas_call x1, Pallas kernels: 43.2 us -> 40.6 us  [shards(): pl.pallas_call(kernel, out_shape=jax.ShapeDtypeStruct((1, 1, CAP, 2, VIS)...]
where the time goes in v4:
time: 43.4 us; the launch traced here: 43.2 us
  Pallas kernels  40.6 us (94%)
  between operations  2 us (5%)
  local copies, waits for them, and re-layouts  0.64 us (1%)
    pallas_call x1, Pallas kernels, shards(): pl.pallas_call(kernel, out_shape=jax.ShapeDtypeStruct((1, 1, CAP, 2, VIS)...  40.6 us

profile of v4, /device:TPU:1, one launch (start us, length us, event | category | flops | bytes accessed | tf_op | source)
XLA Modules:
  0.0 43.2 jit_solution(2530227704427154646)
XLA Ops:
  1.3 0.0 copy-start
  1.3 0.0 copy-start.1
  2.0 0.0 copy-done
  2.0 0.0 copy-done.1
  2.0 40.6 %shard_map.73 = f32[1,1,8,2,1024]{4,3,2,1,0:T(2,128)S(1)} custom-call(bf16[1,2,1024,128]{3,2,1,0:T(8,128)(2,1)} %strip_ref.1, s32[1,2]{1,0:T(1,128)S(1)} %copy-done, s32[1]{0:T(128)S(6)} %copy.9.column_hbm, s32[1]{0:T(128)S(6)} %copy.10.row_hbm, s32[1,1,8]{2,1,0:T(1,128)S(1)} %copy-done.1, s32[1,1]{1,0:T(1,128)S(6)} %copy.11.counts_hbm, ...), custom_call_target="tpu_custom_call" | custom-call | tf_op jit(solution)/shard_map/pallas_call | solution.py:516
  42.6 0.6 %copy.12 = f32[1,1,8,2,1024]{4,3,2,1,0:T(2,128)} copy(f32[1,1,8,2,1024]{4,3,2,1,0:T(2,128)S(1)} %shard_map.73) | data formatting | bytes 131072
Async XLA Ops:
  1.3 0.7 %copy-start = (s32[1,2]{1,0:T(1,128)S(1)}, s32[1,2]{1,0:T(1,128)}, u32[]{:S(2)}) copy-start(s32[1,2]{1,0:T(1,128)} %offsets_hbm.1) | copy-start | bytes 28
  1.3 0.7 %copy-start.1 = (s32[1,1,8]{2,1,0:T(1,128)S(1)}, s32[1,1,8]{2,1,0:T(1,128)}, u32[]{:S(2)}) copy-start(s32[1,1,8]{2,1,0:T(1,128)} %lists_hbm.1) | copy-start | bytes 100

commit v5 on v4

--- a/solution.py
+++ b/solution.py
@@ -19,6 +19,7 @@
 LEN = 1024
 MESH = pl.DeviceIdType.MESH
 DEAL = 0
+LINE = (4, -4, 3, -3, 2, -2)
 ORDER2 = ((0, 2), (0, 1), (0, 3), (1, 2), (0, 0), (1, 1), (1, 3), (1, 0))
 AROUND = (4, -3, 3, -2, 2, -1, 1, 0)
 FAR = ((1, 2), (1, 1), (1, 3), (0, 2), (1, 0), (0, 1), (0, 3))
@@ -104,6 +105,7 @@
     word_2,
     word_3,
     word_4,
+    word_5,
 ):
     facet = lax.axis_index("facet")
     col = lax.axis_index("col")
@@ -146,8 +148,11 @@
     def along(i):
         return facet_of(x_hi, (z + i + 16) % 16, core)
 
-    for i in (4, -4, 3, -3, 2, -2, 2 * zp - 1):
-        greet(along(i), col)
+    def rank(p):
+        return p + 4 * (p // 8 - p // 12) + p // 12 * (23 - 2 * p)
+
+    def is_later(i):
+        return (rank((z + i + 16) % 16) - rank(z) + 15) // 16
 
     @pl.loop(1, 8)
     def _(i):
@@ -156,6 +161,14 @@
     @pl.loop(1, 8)
     def _(i):
         greet(group_facet((g_me + i) % 8, zg), col)
+
+    later = 0
+    for i in LINE + (2 * zp - 1,):
+        later = later + is_later(i)
+
+        @pl.when(is_later(i) == 1)
+        def _():
+            greet(along(i), col)
 
     loads[3].wait()
     loads[4].wait()
@@ -183,7 +196,7 @@
     imag = both[:S, W:] - both[S:, :W]
     send1[...] = jnp.concatenate([real, imag], axis=1).astype(BF16).reshape(8, 32, 2 * W)
 
-    pl.semaphore_wait(barrier, 21)
+    pl.semaphore_wait(barrier, 21 - later)
 
     def copy1(c):
         return pltpu.make_async_remote_copy(
@@ -212,9 +225,11 @@
         def _():
             tell(word_2, group_facet(g, zg))
 
-    tell(word_3, along(4))
-    tell(word_3, along(-4))
-    tell(word_4, facet_of(1 - x_hi, z, core))
+    for i in LINE + (2 * zp - 1,):
+
+        @pl.when(is_later(i) == 0)
+        def _():
+            tell(word_3, along(i))
 
     loads[6].wait()
     loads[7].wait()
@@ -296,6 +311,14 @@
     @pl.when(target == g_me)
     def _():
         recv2[pl.ds(g_me, 1)] = block2[...][None]
+
+    @pl.when(later > 0)
+    def _():
+        pl.semaphore_wait(word_3, later)
+
+    tell(word_5, along(4))
+    tell(word_5, along(-4))
+    tell(word_4, facet_of(1 - x_hi, z, core))
 
     loads[2].wait()
     for part in range(2):
@@ -405,7 +428,7 @@
             device_id=(facet_of(x_hi, 2 * n + zp, core), col), device_id_type=MESH,
         )
 
-    pl.semaphore_wait(word_3, 2)
+    pl.semaphore_wait(word_5, 2)
     for i in (4, 3, 5, 2, 6, 1, 7):
         copy3((zg + i) % 8, zg).start()
 
@@ -564,6 +587,7 @@
             pltpu.SemaphoreType.REGULAR,
             pltpu.SemaphoreType.REGULAR,
             pltpu.SemaphoreType.REGULAR,
+            pltpu.SemaphoreType.REGULAR,
         ],
         compiler_params=pltpu.CompilerParams(
             collective_id=0, has_side_effects=True, vmem_limit_bytes=55104 * 1024

time: 43.4 us -> 43.1 us (level)
  no operation moved by 1% of the time
where the time goes in v5:
time: 43.1 us; the launch traced here: 42.9 us
  Pallas kernels  40.3 us (94%)
  between operations  2 us (5%)
  local copies, waits for them, and re-layouts  0.64 us (1%)
    pallas_call x1, Pallas kernels, shards(): pl.pallas_call(kernel, out_shape=jax.ShapeDtypeStruct((1, 1, CAP, 2, VIS)...  40.3 us

profile of v5, /device:TPU:1, one launch (start us, length us, event | category | flops | bytes accessed | tf_op | source)
XLA Modules:
  0.0 42.9 jit_solution(12269003234963643919)
XLA Ops:
  1.3 0.0 copy-start
  1.3 0.0 copy-start.1
  2.0 0.0 copy-done
  2.0 0.0 copy-done.1
  2.0 40.3 %shard_map.73 = f32[1,1,8,2,1024]{4,3,2,1,0:T(2,128)S(1)} custom-call(bf16[1,2,1024,128]{3,2,1,0:T(8,128)(2,1)} %strip_ref.1, s32[1,2]{1,0:T(1,128)S(1)} %copy-done, s32[1]{0:T(128)S(6)} %copy.9.column_hbm, s32[1]{0:T(128)S(6)} %copy.10.row_hbm, s32[1,1,8]{2,1,0:T(1,128)S(1)} %copy-done.1, s32[1,1]{1,0:T(1,128)S(6)} %copy.11.counts_hbm, ...), custom_call_target="tpu_custom_call" | custom-call | tf_op jit(solution)/shard_map/pallas_call | solution.py:539
  42.3 0.6 %copy.12 = f32[1,1,8,2,1024]{4,3,2,1,0:T(2,128)} copy(f32[1,1,8,2,1024]{4,3,2,1,0:T(2,128)S(1)} %shard_map.73) | data formatting | bytes 131072
Async XLA Ops:
  1.3 0.7 %copy-start = (s32[1,2]{1,0:T(1,128)S(1)}, s32[1,2]{1,0:T(1,128)}, u32[]{:S(2)}) copy-start(s32[1,2]{1,0:T(1,128)} %offsets_hbm.1) | copy-start | bytes 28
  1.3 0.7 %copy-start.1 = (s32[1,1,8]{2,1,0:T(1,128)S(1)}, s32[1,1,8]{2,1,0:T(1,128)}, u32[]{:S(2)}) copy-start(s32[1,1,8]{2,1,0:T(1,128)} %lists_hbm.1) | copy-start | bytes 100

commit v6 on v5

--- a/solution.py
+++ b/solution.py
@@ -20,8 +20,7 @@
 MESH = pl.DeviceIdType.MESH
 DEAL = 0
 LINE = (4, -4, 3, -3, 2, -2)
-ORDER2 = ((0, 2), (0, 1), (0, 3), (1, 2), (0, 0), (1, 1), (1, 3), (1, 0))
-AROUND = (4, -3, 3, -2, 2, -1, 1, 0)
+ORDER2 = ((1, 2), (1, 1), (1, 3), (0, 2), (1, 0), (0, 1), (0, 3), (0, 0))
 FAR = ((1, 2), (1, 1), (1, 3), (0, 2), (1, 0), (0, 1), (0, 3))
 F32 = jnp.float32
 BF16 = jnp.bfloat16
@@ -449,10 +448,16 @@
         )
 
     pl.semaphore_wait(word_4, 1)
-    for i in AROUND:
-        copy4(1, i + 16, 8 + place).start()
-    for i in AROUND[:-1]:
-        copy4(0, i + 16, place).start()
+    def order4(k):
+        return z // 8 * (4 - k) + (1 - z // 8) * (k - 3) + 16
+
+    for x in (1 - core, core):
+        for k in range(8):
+
+            @pl.when((x == 1) | (order4(k) != 16))
+            def _():
+                copy4(x, order4(k), 8 * x + place).start()
+
 
     @pl.loop(0, 8)
     def _(c):

time: 43.1 us -> 43.1 us (level)
  no operation moved by 1% of the time
where the time goes in v6:
time: 43.1 us; the launch traced here: 42.9 us
  Pallas kernels  40.3 us (94%)
  between operations  2 us (5%)
  local copies, waits for them, and re-layouts  0.64 us (1%)
    pallas_call x1, Pallas kernels, shards(): pl.pallas_call(kernel, out_shape=jax.ShapeDtypeStruct((1, 1, CAP, 2, VIS)...  40.3 us

profile of v6, /device:TPU:1, one launch (start us, length us, event | category | flops | bytes accessed | tf_op | source)
XLA Modules:
  0.0 42.9 jit_solution(16622127322630625309)
XLA Ops:
  1.3 0.0 copy-start
  1.3 0.0 copy-start.1
  2.0 0.0 copy-done
  2.0 0.0 copy-done.1
  2.0 40.3 %shard_map.73 = f32[1,1,8,2,1024]{4,3,2,1,0:T(2,128)S(1)} custom-call(bf16[1,2,1024,128]{3,2,1,0:T(8,128)(2,1)} %strip_ref.1, s32[1,2]{1,0:T(1,128)S(1)} %copy-done, s32[1]{0:T(128)S(6)} %copy.9.column_hbm, s32[1]{0:T(128)S(6)} %copy.10.row_hbm, s32[1,1,8]{2,1,0:T(1,128)S(1)} %copy-done.1, s32[1,1]{1,0:T(1,128)S(6)} %copy.11.counts_hbm, ...), custom_call_target="tpu_custom_call" | custom-call | tf_op jit(solution)/shard_map/pallas_call | solution.py:544
  42.3 0.6 %copy.12 = f32[1,1,8,2,1024]{4,3,2,1,0:T(2,128)} copy(f32[1,1,8,2,1024]{4,3,2,1,0:T(2,128)S(1)} %shard_map.73) | data formatting | bytes 131072
Async XLA Ops:
  1.3 0.7 %copy-start = (s32[1,2]{1,0:T(1,128)S(1)}, s32[1,2]{1,0:T(1,128)}, u32[]{:S(2)}) copy-start(s32[1,2]{1,0:T(1,128)} %offsets_hbm.1) | copy-start | bytes 28
  1.3 0.7 %copy-start.1 = (s32[1,1,8]{2,1,0:T(1,128)S(1)}, s32[1,1,8]{2,1,0:T(1,128)}, u32[]{:S(2)}) copy-start(s32[1,1,8]{2,1,0:T(1,128)} %lists_hbm.1) | copy-start | bytes 100

commit v7 on v5

--- a/solution.py
+++ b/solution.py
@@ -397,19 +397,19 @@
     copy_i.wait_send()
 
     terms = None
-    for x in range(2):
-        first = (x_hi + x) % 2 * 4
-
-        @pl.loop(first, first + 4)
+    for x, skip, many in ((0, 0, 4), (1, 0, 2), (1, 2, 2)):
+        first = (x_hi + x) % 2 * 4 + skip
+
+        @pl.loop(first, first + many)
         def _(g):
             @pl.when((target != g_me) | (g != g_me))
             def _():
                 from2(g).wait_recv()
 
         grid = jnp.dot(
-            recv2[pl.ds(first, 4)].reshape(4 * 32, 2 * W), table_v[...], preferred_element_type=F32
-        )
-        for g in range(4):
+            recv2[pl.ds(first, many)].reshape(many * 32, 2 * W), table_v[...], preferred_element_type=F32
+        )
+        for g in range(many):
             rows = grid[32 * g : 32 * g + 32]
             re, im = (turn_v[h, pl.ds(first + g, 1), :] for h in range(2))
             term = rows[:, : 2 * S] * re + rows[:, 2 * S :] * im

time: 43.1 us -> 43 us (level)
  no operation moved by 1% of the time
where the time goes in v7:
time: 43 us; the launch traced here: 42.9 us
  Pallas kernels  40.3 us (94%)
  between operations  2 us (5%)
  local copies, waits for them, and re-layouts  0.64 us (1%)
    pallas_call x1, Pallas kernels, shards(): pl.pallas_call(kernel, out_shape=jax.ShapeDtypeStruct((1, 1, CAP, 2, VIS)...  40.3 us

profile of v7, /device:TPU:1, one launch (start us, length us, event | category | flops | bytes accessed | tf_op | source)
XLA Modules:
  0.0 42.9 jit_solution(12609768183029965507)
XLA Ops:
  1.3 0.0 copy-start
  1.3 0.0 copy-start.1
  2.0 0.0 copy-done
  2.0 0.0 copy-done.1
  2.0 40.3 %shard_map.73 = f32[1,1,8,2,1024]{4,3,2,1,0:T(2,128)S(1)} custom-call(bf16[1,2,1024,128]{3,2,1,0:T(8,128)(2,1)} %strip_ref.1, s32[1,2]{1,0:T(1,128)S(1)} %copy-done, s32[1]{0:T(128)S(6)} %copy.9.column_hbm, s32[1]{0:T(128)S(6)} %copy.10.row_hbm, s32[1,1,8]{2,1,0:T(1,128)S(1)} %copy-done.1, s32[1,1]{1,0:T(1,128)S(6)} %copy.11.counts_hbm, ...), custom_call_target="tpu_custom_call" | custom-call | tf_op jit(solution)/shard_map/pallas_call | solution.py:539
  42.3 0.6 %copy.12 = f32[1,1,8,2,1024]{4,3,2,1,0:T(2,128)} copy(f32[1,1,8,2,1024]{4,3,2,1,0:T(2,128)S(1)} %shard_map.73) | data formatting | bytes 131072
Async XLA Ops:
  1.3 0.7 %copy-start = (s32[1,2]{1,0:T(1,128)S(1)}, s32[1,2]{1,0:T(1,128)}, u32[]{:S(2)}) copy-start(s32[1,2]{1,0:T(1,128)} %offsets_hbm.1) | copy-start | bytes 28
  1.3 0.7 %copy-start.1 = (s32[1,1,8]{2,1,0:T(1,128)S(1)}, s32[1,1,8]{2,1,0:T(1,128)}, u32[]{:S(2)}) copy-start(s32[1,1,8]{2,1,0:T(1,128)} %lists_hbm.1) | copy-start | bytes 100
